TPU v7x, 32 devices: a whole 2x2x4 slice. The times are simulated.
32 devices in a mesh: blk: 8 (over y, x, core), tp: 4 (over z).
Axes of the slice: x: 2, y: 2, z: 4, core: 2. Of those that a mesh axis runs over, the one named last changes fastest.
Arguments:
- hidden_in: bfloat16 [1024, 4, 2048], P('blk'), may hold values from -6 to 6
- block_order: int32 [8], replicated, may hold values from 0 to 7, each once
- seq_labels: int32 [4], replicated, may hold values from 0 to 1
- exit_scales: float32 [2], replicated, may hold values from 0.4 to 2
- attn_gain: bfloat16 [2048], replicated, may hold values from 0.5 to 1.5
- w_query: bfloat16 [2048, 2048], P(None, 'tp'), may hold values from -0.125 to 0.125
- w_key: bfloat16 [2048, 1024], P(None, 'tp'), may hold values from -0.125 to 0.125
- w_value: bfloat16 [2048, 1024], P(None, 'tp'), may hold values from -0.125 to 0.125
- w_out: bfloat16 [2048, 2048], P('tp'), may hold values from -0.5 to 0.5
- mlp_gain: bfloat16 [2048], replicated, may hold values from 0.5 to 1.5
- w_gate: bfloat16 [2048, 5632], P(None, 'tp'), may hold values from -0.125 to 0.125
- w_up: bfloat16 [2048, 5632], P(None, 'tp'), may hold values from -0.125 to 0.125
- w_down: bfloat16 [5632, 2048], P('tp'), may hold values from -0.078125 to 0.078125
- d_out: bfloat16 [1024, 4, 2048], P('blk'), may hold values from -6 to 6
Outputs:
- block_out: bfloat16 [1024, 4, 2048], P('blk')
- d_hidden_in: float32 [1024, 4, 2048], P('blk')
- d_attn_gain: float32 [2048], P('blk')
- d_w_query: float32 [2048, 2048], P('blk', 'tp')
- d_w_key: float32 [2048, 1024], P('blk', 'tp')
- d_w_value: float32 [2048, 1024], P('blk', 'tp')
- d_w_out: float32 [2048, 2048], P('tp', 'blk')
- d_mlp_gain: float32 [2048], P('blk')
- d_w_gate: float32 [2048, 5632], P('blk', 'tp')
- d_w_up: float32 [2048, 5632], P('blk', 'tp')
- d_w_down: float32 [5632, 2048], P('tp', 'blk')
Inputs may be any that keep to these rules, and one draw needn't show every extreme that they name: `block_order`: a permutation: each block of a sequence is held by exactly one index of blk.
All inputs are finite; a program needn't handle non-finite values.
Results may differ from a plain program's by a relative error of at most 0.025.
Values may be sent and summed in bfloat16 or wider, within the bound.
No kernel may reach another device: no remote copies, remote signals or barrier semaphores. Data moves between devices by JAX's collectives and lax.ppermute only.
A program may use at most 256 MiB of HBM per device.

v0:
```python
import math

import jax
import jax.numpy as jnp
from jax import lax
from jax.sharding import PartitionSpec as P

HEAD_DIM = 128


EPS = 1e-05
THETA = 10000.0
NEG = -1e30


def rope_tables(positions, head_dim):
    half = head_dim // 2
    freq = jnp.exp(jnp.arange(half, dtype=jnp.float32) * (-2.0 * math.log(THETA) / head_dim))
    angles = positions.astype(jnp.float32)[:, None] * freq[None, :]
    return (jnp.cos(angles), jnp.sin(angles))


def rotate(values, cosine, sine):
    half = values.shape[-1] // 2
    first = values[..., :half]
    second = values[..., half:]
    cosine = cosine[:, None, None, :]
    sine = sine[:, None, None, :]
    return jnp.concatenate(
        [first * cosine - second * sine, second * cosine + first * sine], axis=-1
    )


def inverse_rms(values):
    return lax.rsqrt(jnp.mean(values * values, axis=-1, keepdims=True) + EPS)


def norm_back(values, inverse, gain, grad):
    unit = values * inverse
    scaled = grad * gain
    back = inverse * (scaled - unit * jnp.mean(scaled * unit, axis=-1, keepdims=True))
    return (back, jnp.sum(grad * unit, axis=(0, 1)))


def matmul(values, weight):
    return jnp.einsum("lsd,de->lse", values, weight, preferred_element_type=jnp.float32)


def matmul_back(values, weight):
    return jnp.einsum("lse,de->lsd", values, weight, preferred_element_type=jnp.float32)


def weight_grad(left, right):
    return jnp.einsum("lsd,lse->de", left, right, preferred_element_type=jnp.float32)


def per_device(
    hidden_in,
    block_order,
    seq_labels,
    exit_scales,
    attn_gain,
    w_query,
    w_key,
    w_value,
    w_out,
    mlp_gain,
    w_gate,
    w_up,
    w_down,
    d_out,
):
    f32 = jnp.float32
    bf16 = jnp.bfloat16
    loc, seqs, width = hidden_in.shape
    head_dim = HEAD_DIM
    q_heads = w_query.shape[1] // head_dim
    kv_heads = w_key.shape[1] // head_dim
    group = q_heads // kv_heads
    scale = head_dim ** (-0.5)
    blocks_all = block_order.shape[0]
    total_rows = loc * lax.axis_size("blk")
    key_rows = math.gcd(512, total_rows)
    block_count = total_rows // key_rows
    kv_width = 2 * kv_heads * head_dim
    positions = block_order[lax.axis_index("blk")] * loc + jnp.arange(loc, dtype=jnp.int32)
    cosine, sine = rope_tables(positions, head_dim)

    def key_positions(start, count):
        index = start + jnp.arange(count, dtype=jnp.int32)
        owner = index // loc
        table = jnp.sum(
            jnp.where(
                owner[:, None] == jnp.arange(blocks_all, dtype=jnp.int32)[None, :],
                block_order[None, :],
                0,
            ),
            axis=1,
        )
        return table * loc + index % loc

    xin = hidden_in.astype(f32)
    inv_a = inverse_rms(xin)
    gain_a = attn_gain.astype(f32)
    normed = (xin * inv_a * gain_a).astype(bf16)
    query_bf = rotate(
        matmul(normed, w_query).reshape(loc, seqs, q_heads, head_dim), cosine, sine
    ).astype(bf16)
    keys_bf = (
        rotate(matmul(normed, w_key).reshape(loc, seqs, kv_heads, head_dim), cosine, sine)
        .astype(bf16)
        .reshape(loc, seqs, kv_heads * head_dim)
    )
    vals_bf = matmul(normed, w_value).astype(bf16)
    query_g = query_bf.reshape(loc, seqs, kv_heads, group, head_dim)
    starts = jnp.arange(block_count, dtype=jnp.int32) * key_rows
    top = jnp.full((seqs, kv_heads, group, loc), NEG, f32)
    key_part = lax.all_gather(keys_bf, "blk", axis=0, tiled=True)
    val_part = lax.all_gather(vals_bf, "blk", axis=0, tiled=True)
    count = key_part.shape[0]
    kk = key_part.reshape(count, seqs, kv_heads, head_dim)
    vv = val_part.reshape(count, seqs, kv_heads, head_dim)
    mask = key_positions(jnp.int32(0), count)[None, :] <= positions[:, None]
    raw = jnp.einsum("lsngd,msnd->snglm", query_g, kk, preferred_element_type=f32)
    scores = jnp.where(mask, raw * scale, NEG)
    new_top = jnp.maximum(top, jnp.max(scores, axis=-1))
    weights = jnp.where(mask, jnp.exp(scores - new_top[..., None]), 0.0)
    total = jnp.sum(weights, axis=-1)
    acc = jnp.einsum("snglm,msnd->sngld", weights.astype(bf16), vv, preferred_element_type=f32)
    top, total, acc = (new_top, total, acc)
    lse = top + jnp.log(total)
    mixed_raw = acc / total[..., None]
    mixed_bf = (
        mixed_raw.transpose(3, 0, 1, 2, 4).reshape(loc, seqs, q_heads * head_dim).astype(bf16)
    )
    resid = xin + lax.psum(matmul(mixed_bf, w_out).astype(jnp.bfloat16), "tp").astype(jnp.float32)
    inv_m = inverse_rms(resid)
    gain_m = mlp_gain.astype(f32)
    normed_m = (resid * inv_m * gain_m).astype(bf16)
    gate = matmul(normed_m, w_gate)
    up = matmul(normed_m, w_up)
    sig = jax.nn.sigmoid(gate)
    silu = gate * sig
    hidden = (silu * up).astype(bf16)
    output = resid + lax.psum(matmul(hidden, w_down).astype(jnp.bfloat16), "tp").astype(jnp.float32)
    block_out = output.astype(bf16)
    scale_rows = jnp.where(seq_labels == 1, exit_scales[1], exit_scales[0])
    cot = d_out.astype(f32) * scale_rows[None, :, None]
    g_down = cot.astype(bf16)
    d_w_down = weight_grad(hidden, g_down)
    d_hidden = matmul_back(g_down, w_down)
    g_up = (d_hidden * silu).astype(bf16)
    g_gate = (d_hidden * up * (sig * (1.0 + gate * (1.0 - sig)))).astype(bf16)
    d_w_gate = weight_grad(normed_m, g_gate)
    d_w_up = weight_grad(normed_m, g_up)
    d_nm = lax.psum(
        (matmul_back(g_gate, w_gate) + matmul_back(g_up, w_up)).astype(jnp.bfloat16), "tp"
    ).astype(jnp.float32)
    d_resid_norm, d_mlp_gain = norm_back(resid, inv_m, gain_m, d_nm)
    d_resid = cot + d_resid_norm
    g_attn = d_resid.astype(bf16)
    d_w_out = weight_grad(mixed_bf, g_attn)
    g_mixed = matmul_back(g_attn, w_out).astype(bf16)
    g_mixed_g = g_mixed.reshape(loc, seqs, kv_heads, group, head_dim)
    delta = jnp.sum(g_mixed_g.astype(f32).transpose(1, 2, 3, 0, 4) * mixed_raw, axis=-1)
    whole_keys, whole_vals = (
        lax.all_gather(keys_bf, "blk", axis=0, tiled=True),
        lax.all_gather(vals_bf, "blk", axis=0, tiled=True),
    )

    def probe(kk, vv, start, count):
        mask = key_positions(start, count)[None, :] <= positions[:, None]
        raw = jnp.einsum("lsngd,msnd->snglm", query_g, kk, preferred_element_type=f32)
        probs = jnp.where(mask, jnp.exp(raw * scale - lse[..., None]), 0.0)
        d_probs = jnp.einsum("lsngd,msnd->snglm", g_mixed_g, vv, preferred_element_type=f32)
        g_scores = (probs * (d_probs - delta[..., None]) * scale).astype(bf16)
        return (g_scores, probs)

    def kv_pair(g_scores, probs, count):
        d_keys = jnp.einsum("snglm,lsngd->msnd", g_scores, query_g, preferred_element_type=f32)
        d_vals = jnp.einsum(
            "snglm,lsngd->msnd", probs.astype(bf16), g_mixed_g, preferred_element_type=f32
        )
        return jnp.concatenate([d_keys, d_vals], axis=2).reshape(count, seqs, kv_width)

    scan_items = (
        whole_keys.reshape(block_count, key_rows, seqs, -1),
        whole_vals.reshape(block_count, key_rows, seqs, -1),
        starts,
    )
    zero_query = jnp.zeros((loc, seqs, kv_heads, group, head_dim), f32)

    def back_step(d_query, item):
        key_part, val_part, start = item
        kk = key_part.reshape(key_rows, seqs, kv_heads, head_dim)
        vv = val_part.reshape(key_rows, seqs, kv_heads, head_dim)
        g_scores, probs = probe(kk, vv, start, key_rows)
        d_query = d_query + jnp.einsum(
            "snglm,msnd->lsngd", g_scores, kk, preferred_element_type=f32
        )
        return (d_query, kv_pair(g_scores, probs, key_rows))

    d_query, kv_terms = lax.scan(back_step, zero_query, scan_items)
    kv_local = lax.psum_scatter(
        kv_terms.reshape(total_rows, seqs, kv_width).astype(jnp.bfloat16),
        "blk",
        scatter_dimension=0,
        tiled=True,
    ).astype(jnp.float32)
    kv_local = kv_local.reshape(loc, seqs, 2, kv_heads, head_dim)
    g_q = (
        rotate(d_query.reshape(loc, seqs, q_heads, head_dim), cosine, -sine)
        .astype(bf16)
        .reshape(loc, seqs, q_heads * head_dim)
    )
    g_k = (
        rotate(kv_local[:, :, 0], cosine, -sine)
        .astype(bf16)
        .reshape(loc, seqs, kv_heads * head_dim)
    )
    g_v = kv_local[:, :, 1].astype(bf16).reshape(loc, seqs, kv_heads * head_dim)
    d_w_query = weight_grad(normed, g_q)
    d_w_key = weight_grad(normed, g_k)
    d_w_value = weight_grad(normed, g_v)
    d_n = lax.psum(
        (matmul_back(g_q, w_query) + matmul_back(g_k, w_key) + matmul_back(g_v, w_value)).astype(
            jnp.bfloat16
        ),
        "tp",
    ).astype(jnp.float32)
    d_in_norm, d_attn_gain = norm_back(xin, inv_a, gain_a, d_n)
    d_hidden_in = d_resid + d_in_norm
    d_attn_gain, d_w_query, d_w_key, d_w_value, d_w_out, d_mlp_gain, d_w_gate, d_w_up, d_w_down = (
        lax.psum_scatter(
            d_attn_gain.astype(jnp.bfloat16), "blk", scatter_dimension=0, tiled=True
        ).astype(jnp.float32),
        lax.psum_scatter(
            d_w_query.astype(jnp.bfloat16), "blk", scatter_dimension=0, tiled=True
        ).astype(jnp.float32),
        lax.psum_scatter(
            d_w_key.astype(jnp.bfloat16), "blk", scatter_dimension=0, tiled=True
        ).astype(jnp.float32),
        lax.psum_scatter(
            d_w_value.astype(jnp.bfloat16), "blk", scatter_dimension=0, tiled=True
        ).astype(jnp.float32),
        lax.psum_scatter(
            d_w_out.astype(jnp.bfloat16), "blk", scatter_dimension=1, tiled=True
        ).astype(jnp.float32),
        lax.psum_scatter(
            d_mlp_gain.astype(jnp.bfloat16), "blk", scatter_dimension=0, tiled=True
        ).astype(jnp.float32),
        lax.psum_scatter(
            d_w_gate.astype(jnp.bfloat16), "blk", scatter_dimension=0, tiled=True
        ).astype(jnp.float32),
        lax.psum_scatter(
            d_w_up.astype(jnp.bfloat16), "blk", scatter_dimension=0, tiled=True
        ).astype(jnp.float32),
        lax.psum_scatter(
            d_w_down.astype(jnp.bfloat16), "blk", scatter_dimension=1, tiled=True
        ).astype(jnp.float32),
    )
    return (
        block_out,
        d_hidden_in,
        d_attn_gain,
        d_w_query,
        d_w_key,
        d_w_value,
        d_w_out,
        d_mlp_gain,
        d_w_gate,
        d_w_up,
        d_w_down,
    )


def solution(mesh):
    return jax.shard_map(
        per_device,
        mesh=mesh,
        in_specs=(
            P("blk", None, None),
            P(),
            P(),
            P(),
            P(),
            P(None, "tp"),
            P(None, "tp"),
            P(None, "tp"),
            P("tp", None),
            P(),
            P(None, "tp"),
            P(None, "tp"),
            P("tp", None),
            P("blk", None, None),
        ),
        out_specs=(
            P("blk", None, None),
            P("blk", None, None),
            P("blk"),
            P("blk", "tp"),
            P("blk", "tp"),
            P("blk", "tp"),
            P("tp", "blk"),
            P("blk"),
            P("blk", "tp"),
            P("blk", "tp"),
            P("tp", "blk"),
        ),
        check_vma=False,
    )
```

profile of v0, /device:TPU:0, one launch (start us, length us, event | category | flops | bytes accessed | tf_op | source)
XLA Modules:
  0.0 966.5 jit_solution(8049662194071616949)
XLA Ops:
  13.7 4.5 fusion.85
  19.1 4.7 convolution_convert_fusion.1
  24.6 5.8 fusion.73
  33.5 16.5 %all-gather.3.cloned.1.call-done = bf16[1024,4,256]{0,2,1:T(8,128)(2,1)} async-done(((bf16[128,4,256]{0,2,1:T(8,128)(2,1)}), bf16[1024,4,256]{0,2,1:T(8,128)(2,1)}) %all-gather.3.cloned.1.call-update) | async-done | bytes 2097168 | tf_op jit(solution)/shard_map/all_gather | solution.py:118
  58.5 22.0 %all-gather.5.cloned.1.call-done = bf16[1024,4,256]{2,0,1:T(8,128)(2,1)} async-done(((bf16[128,4,256]{2,0,1:T(8,128)(2,1)}), bf16[1024,4,256]{2,0,1:T(8,128)(2,1)}) %all-gather.5.cloned.1.call-update) | async-done | bytes 2097168 | tf_op jit(solution)/shard_map/all_gather | solution.py:119
  84.4 7.0 fusion.79
  97.0 9.7 %fusion.31 = f32[128,4,1408]{2,0,1:T(8,128)} fusion(bf16[1408,2048]{1,0:T(8,128)(2,1)} %param.28, f32[4]{0:T(128)S(1)} %compare_select_fusion, bf16[128,4,2048]{2,1,0:T(4,128)(2,1)} %param.29), kind=kOutput, calls=%fused_computation.54 | convolution fusion | flops 2955935744 | bytes 10747920 | tf_op jit(solution)/shard_map/lse,de->lsd/dot_general | solution.py:50
  106.7 74.8 %all-reduce.8.cloned.1.call-done = bf16[128,4,2048]{2,0,1:T(8,128)(2,1)} async-done(((bf16[128,4,2048]{2,0,1:T(8,128)(2,1)}), bf16[128,4,2048]{2,0,1:T(8,128)(2,1)}) %all-reduce.8.cloned.1.call-update) | async-done | bytes 2097168 | tf_op jit(solution)/shard_map/psum | solution.py:136
  186.9 6.9 fusion.37
  193.9 5.6 multiply_convert_fusion.2
  202.9 4.7 add_convert_fusion.1
  211.4 81.9 %all-reduce.10.cloned.1.call-done = bf16[128,4,2048]{2,0,1:T(8,128)(2,1)} async-done(((bf16[128,4,2048]{2,0,1:T(8,128)(2,1)}), bf16[128,4,2048]{2,0,1:T(8,128)(2,1)}) %all-reduce.10.cloned.1.call-update) | async-done | bytes 2097168 | tf_op jit(solution)/shard_map/psum | solution.py:156
  293.2 5.7 fusion.51
  298.9 8.1 fusion.75
  309.7 51.9 %while.15 = (s32[]{:T(128)}, f32[128,4,2,2,128]{0,4,3,2,1:T(8,128)}, bf16[2,512,4,512]{3,1,0,2:T(8,128)(2,1)}, bf16[2,512,4,256]{1,3,2,0:T(8,128)(2,1)}, s32[2]{...) while((s32[]{:T(128)}, ...), condition=%wide.region_12.13_spmd.clone, body=%wide.region_10.12_spmd.clone.sunk | while | flops 1355377280 | bytes 89364312 | solution.py:203
  363.2 10.1 %bitcast_convert_fusion.3 = bf16[512,2048]{1,0:T(8,128)(2,1)} fusion(bf16[128,4,512]{0,2,1:T(8,128)(2,1)} %bitcast.262, bf16[128,4,2048]{2,0,1:T(8,128)(2,1)} %all-reduce.10.cloned.1.call-done, bf16[128,4,2048]{2,0,1:T(8,128)(2,1)} %all-reduce.8.cloned.1.call-done, f32[128,4]{0,1:T(4,128)S(1)} %broadcast_multiply_fusion.1, f32[4]{0:T(128)S(1)} %compare_select_fusion, ...), kind=kOutput, calls=%fused_computation.82 | convolution fusion | flops 1088421888 | bytes 11022352 | tf_op jit(solution)/shard_map/lsd,lse->de/dot_general | solution.py:54
  385.4 8.0 bitcast_convert_fusion.2
  393.5 8.0 bitcast_convert_fusion.1
  401.8 9.8 %bitcast_convert_fusion = bf16[1408,2048]{1,0:T(8,128)(2,1)} fusion(bf16[128,4,1408]{2,0,1:T(8,128)(2,1)} %get-tuple-element.334, f32[4]{0:T(128)S(1)} %compare_select_fusion, bf16[128,4,2048]{2,1,0:T(4,128)(2,1)} %param.29), kind=kOutput, calls=%fused_computation.39 | convolution fusion | flops 2958819328 | bytes 9306128 | tf_op jit(solution)/shard_map/lsd,lse->de/dot_general | solution.py:54
  421.5 8.3 fusion.63
  436.4 20.5 %reduce-scatter.17.cloned.1.call-done = bf16[512,256]{1,0:T(8,128)(2,1)} async-done(((bf16[512,2048]{1,0:T(8,128)(2,1)}), bf16[512,256]{1,0:T(8,128)(2,1)}) %reduce-scatter.17.cloned.1.call-update) | async-done | bytes 262160 | tf_op jit(solution)/shard_map/reduce_scatter | solution.py:246
  458.6 42.7 %reduce-scatter.11.cloned.1.call-done = bf16[256,512]{1,0:T(8,128)(2,1)} async-done(((bf16[2048,512]{1,0:T(8,128)(2,1)}), bf16[256,512]{1,0:T(8,128)(2,1)}) %reduce-scatter.11.cloned.1.call-update) | async-done | bytes 262160 | tf_op jit(solution)/shard_map/reduce_scatter | solution.py:237
  503.2 61.1 %reduce-scatter.19.cloned.1.call-done = bf16[256,1408]{1,0:T(8,128)(2,1)} async-done(((bf16[2048,1408]{1,0:T(8,128)(2,1)}), bf16[256,1408]{1,0:T(8,128)(2,1)}) %reduce-scatter.19.cloned.1.call-update) | async-done | bytes 720912 | tf_op jit(solution)/shard_map/reduce_scatter | solution.py:252
  566.6 60.2 %reduce-scatter.21.cloned.1.call-done = bf16[256,1408]{1,0:T(8,128)(2,1)} async-done(((bf16[2048,1408]{1,0:T(8,128)(2,1)}), bf16[256,1408]{1,0:T(8,128)(2,1)}) %reduce-scatter.21.cloned.1.call-update) | async-done | bytes 720912 | tf_op jit(solution)/shard_map/reduce_scatter | solution.py:255
  629.1 60.4 %reduce-scatter.23.cloned.1.call-done = bf16[1408,256]{1,0:T(8,128)(2,1)} async-done(((bf16[1408,2048]{1,0:T(8,128)(2,1)}), bf16[1408,256]{1,0:T(8,128)(2,1)}) %reduce-scatter.23.cloned.1.call-update) | async-done | bytes 720912 | tf_op jit(solution)/shard_map/reduce_scatter | solution.py:258
  691.9 36.9 %reduce-scatter.13.cloned.1.call-done = bf16[256,256]{1,0:T(8,128)(2,1)} async-done(((bf16[2048,256]{1,0:T(8,128)(2,1)}), bf16[256,256]{1,0:T(8,128)(2,1)}) %reduce-scatter.13.cloned.1.call-update) | async-done | bytes 131088 | tf_op jit(solution)/shard_map/reduce_scatter | solution.py:240
  730.4 37.4 %reduce-scatter.15.cloned.1.call-done = bf16[256,256]{1,0:T(8,128)(2,1)} async-done(((bf16[2048,256]{1,0:T(8,128)(2,1)}), bf16[256,256]{1,0:T(8,128)(2,1)}) %reduce-scatter.15.cloned.1.call-update) | async-done | bytes 131088 | tf_op jit(solution)/shard_map/reduce_scatter | solution.py:243
  769.5 156.7 %all-reduce.12.cloned.1.call-done = (bf16[128,4,2048]{2,0,1:T(8,128)(2,1)}, bf16[128,4,2048]{2,0,1:T(8,128)(2,1)}) async-done(((bf16[128,4,2048]{2,0,1:T(8,128)(2,1)}, bf16[128,4,2048]{2,0,1:T(8,128)(2,1)}), (bf16[128,4,2048]{2,0,1:T(8,128)(2,1)}, bf16[128,4,2048]{2,0,1:T(8,128)(2,1)})) %all-reduce.12.cloned.1.call-update) | async-done | bytes 4194320 | tf_op jit(solution)/shard_map/psum | solution.py:145
  926.2 4.3 fusion.54
  930.5 7.0 fusion.47
  937.6 4.7 copy.165
  945.2 13.9 %all-reduce.2 = (bf16[2048]{0:T(1024)(128)(2,1)S(1)}, bf16[2048]{0:T(1024)(128)(2,1)S(1)}) all-reduce(bf16[2048]{0:T(1024)(128)(2,1)S(1)} %get-tuple-element.302, bf16[2048]{0:T(1024)(128)(2,1)S(1)} %get-tuple-element.300), channel_id=3, replica_groups=mesh['blk'=8,'tp'=4] {'blk'}, use_global_device_ids=true, to_apply=%region_17.18.clone | all-reduce | flops 4096 | bytes 16384
  (219 shorter events, 141.8 us)
Async XLA Ops:
  7.2 85.0 %copy-start = (bf16[512,2048]{1,0:T(8,128)(2,1)S(1)}, bf16[512,2048]{1,0:T(8,128)(2,1)}, u32[]{:S(2)}) copy-start(bf16[512,2048]{1,0:T(8,128)(2,1)} %param.24) | copy-start | bytes 6291460
  7.2 42.9 %all-gather.3.cloned.1.call-start = ((), (), s32[]{:S(2)}) async-start(), calls=%async_computation.8 | async-start | bytes 2359296 | tf_op jit(solution)/shard_map/all_gather | solution.py:118
  10.8 8.2 copy-start.20
  13.7 10.7 %copy-start.23 = (f32[128,64]{0,1:T(8,128)}, f32[128,64]{0,1:T(8,128)S(1)}, u32[]{:S(2)}) copy-start(f32[128,64]{0,1:T(8,128)S(1)} %get-tuple-element.351) | copy-start | bytes 98308
  19.0 61.5 %all-gather.5.cloned.1.call-start = ((), (), s32[]{:S(2)}) async-start(), calls=%async_computation.9 | async-start | bytes 2359296 | tf_op jit(solution)/shard_map/all_gather | solution.py:119
  23.8 157.7 %all-reduce.8.cloned.1.call-start = ((), (), s32[]{:S(2)}) async-start(), calls=%async_computation.10 | async-start | bytes 4194304 | tf_op jit(solution)/shard_map/psum | solution.py:136
  94.9 198.4 %all-reduce.10.cloned.1.call-start = ((), (), s32[]{:S(2)}) async-start(), calls=%async_computation.11 | async-start | bytes 4194304 | tf_op jit(solution)/shard_map/psum | solution.py:156
  185.2 8.6 slice-start.2
  186.9 6.9 copy-start.18
  186.9 6.9 slice-start.3
  186.9 6.9 copy-start.31
  186.9 12.5 %slice-start = ((s8[5767168]{0:T(1024)(128)(4,1)}), s8[4194304]{0:T(1024)(128)(4,1)S(1)}, s32[]{:S(2)}) async-start(s8[5767168]{0:T(1024)(128)(4,1)} %bitcast.265), calls=%async_computation.21 | async-start | bytes 8388608
  193.8 5.6 slice-start.1
  207.6 204.5 %reduce-scatter.9.cloned.1.call-start = ((), (), s32[]{:S(2)}) async-start(), calls=%async_computation.12 | async-start | bytes 4718592 | tf_op jit(solution)/shard_map/reduce_scatter | solution.py:204
  293.2 5.7 copy-start.5
  293.2 5.7 copy-start.11
  293.2 5.7 copy-start.15
  317.8 5.1 copy-start.2
  325.4 7.3 copy-start.7
  351.1 7.3 copy-start.7
  361.7 11.9 %copy-start.25 = (f32[128,64]{0,1:T(8,128)S(1)}, f32[128,64]{0,1:T(8,128)}, u32[]{:S(2)}) copy-start(f32[128,64]{0,1:T(8,128)} %get-tuple-element.349) | copy-start | bytes 98308
  361.7 12.0 %copy-start.9 = (f32[128,4,2,2,128]{0,4,3,2,1:T(8,128)S(1)}, f32[128,4,2,2,128]{0,4,3,2,1:T(8,128)}, u32[]{:S(2)}) copy-start(f32[128,4,2,2,128]{0,4,3,2,1:T(8,128)} %get-tuple-element.164) | copy-start | bytes 3145732
  361.7 95.2 %reduce-scatter.17.cloned.1.call-start = ((), (), s32[]{:S(2)}) async-start(), calls=%async_computation.16 | async-start | bytes 2359296 | tf_op jit(solution)/shard_map/reduce_scatter | solution.py:246
  373.3 128.0 %reduce-scatter.11.cloned.1.call-start = ((), (), s32[]{:S(2)}) async-start(), calls=%async_computation.13 | async-start | bytes 2359296 | tf_op jit(solution)/shard_map/reduce_scatter | solution.py:237
  385.4 178.9 %reduce-scatter.19.cloned.1.call-start = ((), (), s32[]{:S(2)}) async-start(), calls=%async_computation.17 | async-start | bytes 6488064 | tf_op jit(solution)/shard_map/reduce_scatter | solution.py:252
  393.4 233.4 %reduce-scatter.21.cloned.1.call-start = ((), (), s32[]{:S(2)}) async-start(), calls=%async_computation.18 | async-start | bytes 6488064 | tf_op jit(solution)/shard_map/reduce_scatter | solution.py:255
  401.5 288.0 %reduce-scatter.23.cloned.1.call-start = ((), (), s32[]{:S(2)}) async-start(), calls=%async_computation.19 | async-start | bytes 6488064 | tf_op jit(solution)/shard_map/reduce_scatter | solution.py:258
  411.6 317.2 %reduce-scatter.13.cloned.1.call-start = ((), (), s32[]{:S(2)}) async-start(), calls=%async_computation.14 | async-start | bytes 1179648 | tf_op jit(solution)/shard_map/reduce_scatter | solution.py:240
  417.3 350.5 %reduce-scatter.15.cloned.1.call-start = ((), (), s32[]{:S(2)}) async-start(), calls=%async_computation.15 | async-start | bytes 1179648 | tf_op jit(solution)/shard_map/reduce_scatter | solution.py:243
  421.0 505.1 %all-reduce.12.cloned.1.call-start = ((), (), s32[]{:S(2)}) async-start(), calls=%async_computation.20 | async-start | bytes 8388608 | tf_op jit(solution)/shard_map/psum | solution.py:145
  421.5 8.3 copy-start.19
  937.5 22.2 %copy-start.1 = (bf16[512,2048]{1,0:T(8,128)(2,1)S(1)}, bf16[512,2048]{1,0:T(8,128)(2,1)}, u32[]{:S(2)}) copy-start(bf16[512,2048]{1,0:T(8,128)(2,1)} %param.24) | copy-start | bytes 6291460
  (24 other events, 64.7 us)
Sparse Core Ops, SparseCore 0:
  19.1 30.8 all-gather.2
  52.5 27.8 all-gather.4
  95.0 86.5 all-reduce.7
  207.8 85.4 all-reduce.9
  361.8 50.2 reduce-scatter.8
  415.6 41.2 reduce-scatter.16
  460.1 41.1 reduce-scatter.10
  505.2 59.0 reduce-scatter.18
  567.7 59.0 reduce-scatter.20
  630.5 59.0 reduce-scatter.22
  692.7 35.9 reduce-scatter.12
  731.8 35.9 reduce-scatter.14
  770.8 155.3 all-reduce.11
where the time goes:
time: 973 us; the launch traced here: 966 us
  waiting for transfers between devices  672 us (69%)
  matrix products  148 us (15%)
  local copies, waits for them, and re-layouts  57 us (6%)
  other arithmetic  56.7 us (6%)
  between operations  16 us (2%)
  blocking collectives  13.9 us (1%)
    psum x1, waiting for transfers between devices, per_device(): lax.psum(matmul(hidden, w_down).astype(jnp.bfloat16), 'tp')  157 us
    psum x1, waiting for transfers between devices, per_device(): lax.psum((matmul_back(g_gate, w_gate) + matmul_back(g_up, w_up)).astype(j...  81.9 us
    psum x1, waiting for transfers between devices, per_device(): lax.psum(matmul(mixed_bf, w_out).astype(jnp.bfloat16), 'tp')  74.8 us
    reduce_scatter x1, waiting for transfers between devices, per_device(): lax.psum_scatter(d_w_gate.astype(jnp.bfloat16), 'blk', scatter_dimension=...  61.1 us
    reduce_scatter x1, waiting for transfers between devices, per_device(): lax.psum_scatter(d_w_down.astype(jnp.bfloat16), 'blk', scatter_dimension=...  60.4 us
    reduce_scatter x1, waiting for transfers between devices, per_device(): lax.psum_scatter(d_w_up.astype(jnp.bfloat16), 'blk', scatter_dimension=0,...  60.2 us
    dot_general x7, matrix products, weight_grad(): jnp.einsum('lsd,lse->de', left, right, preferred_element_type=jnp.float32)  47.3 us
    reduce_scatter x1, waiting for transfers between devices, per_device(): lax.psum_scatter(d_w_query.astype(jnp.bfloat16), 'blk', scatter_dimension...  42.7 us
  transfers between devices with their start and end apart: 13, of which 13 were waited for; matrix products, arithmetic and copies ran while one was open for 12% of the time, Pallas kernels for 0%

commit v1 on v0

--- a/solution.py
+++ b/solution.py
@@ -1,16 +1,217 @@
+import functools
 import math
 
 import jax
 import jax.numpy as jnp
 from jax import lax
+from jax.experimental import pallas as pl
+from jax.experimental.pallas import tpu as pltpu
 from jax.sharding import PartitionSpec as P
 
 HEAD_DIM = 128
-
-
 EPS = 1e-05
 THETA = 10000.0
 NEG = -1e30
+F32 = jnp.float32
+BF16 = jnp.bfloat16
+MIB = 1024 * 1024
+
+
+def dot(left, right):
+    return lax.dot_general(left, right, (((1,), (0,)), ((), ())), preferred_element_type=F32)
+
+
+def dot_rt(left, right):
+    return lax.dot_general(left, right, (((1,), (1,)), ((), ())), preferred_element_type=F32)
+
+
+def dot_lt(left, right):
+    return lax.dot_general(left, right, (((0,), (0,)), ((), ())), preferred_element_type=F32)
+
+
+def params(limit):
+    return pltpu.CompilerParams(vmem_limit_bytes=limit * MIB)
+
+
+def cost(flops, moved):
+    return pl.CostEstimate(flops=int(flops), bytes_accessed=int(moved), transcendentals=0)
+
+
+SMEM = pl.BlockSpec(memory_space=pltpu.SMEM)
+VMEM = pl.BlockSpec(memory_space=pltpu.VMEM)
+
+
+def project_kernel(heads, kv, x_ref, gain_ref, cos_ref, sin_ref, wq_ref, wk_ref, wv_ref, msg_ref, norm_ref):
+    group = heads // kv
+    seqs, loc, width = x_ref.shape
+    gain = gain_ref[...].astype(F32)
+    for s in range(seqs):
+        x = x_ref[s].astype(F32)
+        inv = lax.rsqrt(jnp.mean(x * x, axis=-1, keepdims=True) + EPS)
+        norm_ref[s] = (x * inv * gain).astype(BF16)
+    normed = norm_ref[...].reshape(seqs * loc, width)
+    cosine, sine = cos_ref[...], sin_ref[...]
+
+    def rot(t):
+        return (t * cosine + pltpu.roll(t, HEAD_DIM // 2, 1) * sine).astype(BF16)
+
+    def put(res, h, s, n, slot, turn):
+        part = res[s * loc:(s + 1) * loc, h * HEAD_DIM:(h + 1) * HEAD_DIM]
+        msg_ref[s * kv + n, :, slot * HEAD_DIM:(slot + 1) * HEAD_DIM] = rot(part) if turn else part.astype(BF16)
+
+    query = dot(normed, wq_ref[...])
+    for s in range(seqs):
+        for h in range(heads):
+            put(query, h, s, h // group, h % group, True)
+    keys = dot(normed, wk_ref[...])
+    for s in range(seqs):
+        for n in range(kv):
+            put(keys, n, s, n, group, True)
+    vals = dot(normed, wv_ref[...])
+    for s in range(seqs):
+        for n in range(kv):
+            put(vals, n, s, n, group + 1, False)
+
+
+def project(x, gain, cosine, sine, wq, wk, wv):
+    seqs, loc, width = x.shape
+    heads, kv = wq.shape[1] // HEAD_DIM, wk.shape[1] // HEAD_DIM
+    cols = (heads // kv + 2) * HEAD_DIM
+    flops = 2 * seqs * loc * width * (wq.shape[1] + 2 * wk.shape[1])
+    return pl.pallas_call(
+        functools.partial(project_kernel, heads, kv),
+        out_shape=(jax.ShapeDtypeStruct((seqs * kv, loc, cols), BF16), jax.ShapeDtypeStruct(x.shape, BF16)),
+        in_specs=[VMEM] * 7,
+        out_specs=(VMEM, VMEM),
+        compiler_params=params(32),
+        cost_estimate=cost(flops, 12 * MIB),
+    )(x, gain, cosine, sine, wq, wk, wv)
+
+
+def attend_kernel(group, at_ref, rec_ref, out_ref, full_ref, lse_ref, keys, vals):
+    blocks, loc, _ = rec_ref.shape
+    base = group * HEAD_DIM
+    for p in range(blocks):
+        i = at_ref[p]
+        keys[p * loc:(p + 1) * loc, :] = rec_ref[i, :, base:base + HEAD_DIM]
+        vals[p * loc:(p + 1) * loc, :] = rec_ref[i, :, base + HEAD_DIM:base + 2 * HEAD_DIM]
+    rows = lax.broadcasted_iota(jnp.int32, (group * loc, loc), 0) % loc
+    cols = lax.broadcasted_iota(jnp.int32, (group * loc, loc), 1)
+    keep = cols <= rows
+    for p in range(blocks):
+        i = at_ref[p]
+        count = (p + 1) * loc
+        query = jnp.concatenate([rec_ref[i, :, g * HEAD_DIM:(g + 1) * HEAD_DIM] for g in range(group)], axis=0)
+        scores = dot_rt(query, keys[:count, :]) * (HEAD_DIM ** -0.5)
+        last = jnp.where(keep, scores[:, count - loc:], NEG)
+        scores = jnp.concatenate([scores[:, :count - loc], last], axis=1) if p else last
+        top = jnp.max(scores, axis=-1, keepdims=True)
+        weights = jnp.exp(scores - top)
+        total = jnp.sum(weights, axis=-1, keepdims=True)
+        mixed = dot(weights.astype(BF16), vals[:count, :]) / total
+        lse_ref[p] = jnp.broadcast_to(top + jnp.log(total), (group * loc, HEAD_DIM))
+        full_ref[p] = mixed
+        for g in range(group):
+            out_ref[i, :, g * HEAD_DIM:(g + 1) * HEAD_DIM] = mixed[g * loc:(g + 1) * loc].astype(BF16)
+
+
+def attend(at, rec, group):
+    blocks, loc, _ = rec.shape
+    total = blocks * loc
+    return pl.pallas_call(
+        functools.partial(attend_kernel, group),
+        out_shape=(
+            jax.ShapeDtypeStruct((blocks, loc, group * HEAD_DIM), BF16),
+            jax.ShapeDtypeStruct((blocks, group * loc, HEAD_DIM), F32),
+            jax.ShapeDtypeStruct((blocks, group * loc, HEAD_DIM), F32),
+        ),
+        in_specs=[SMEM, VMEM],
+        out_specs=(VMEM,) * 3,
+        scratch_shapes=[pltpu.VMEM((total, HEAD_DIM), BF16)] * 2,
+        compiler_params=params(32),
+        cost_estimate=cost(3 * group * total * total * HEAD_DIM, 4 * MIB),
+    )(at, rec)
+
+
+def attend_back_kernel(group, at_ref, rec_ref, grad_ref, full_ref, lse_ref, cos_ref, sin_ref, out_ref, keys, vals, d_keys, d_vals):
+    blocks, loc, _ = rec_ref.shape
+    base = group * HEAD_DIM
+    scale = HEAD_DIM ** -0.5
+    for p in range(blocks):
+        i = at_ref[p]
+        keys[p * loc:(p + 1) * loc, :] = rec_ref[i, :, base:base + HEAD_DIM]
+        vals[p * loc:(p + 1) * loc, :] = rec_ref[i, :, base + HEAD_DIM:base + 2 * HEAD_DIM]
+    rows = lax.broadcasted_iota(jnp.int32, (group * loc, loc), 0) % loc
+    cols = lax.broadcasted_iota(jnp.int32, (group * loc, loc), 1)
+    keep = cols <= rows
+
+    def unrot(t, cosine, sine):
+        return (t * cosine - pltpu.roll(t, HEAD_DIM // 2, 1) * sine).astype(BF16)
+
+    for p in reversed(range(blocks)):
+        i = at_ref[p]
+        count = (p + 1) * loc
+        span = slice(p * loc, count)
+        query = jnp.concatenate([rec_ref[i, :, g * HEAD_DIM:(g + 1) * HEAD_DIM] for g in range(group)], axis=0)
+        grad = jnp.concatenate([grad_ref[i, :, g * HEAD_DIM:(g + 1) * HEAD_DIM] for g in range(group)], axis=0)
+        lse = lse_ref[p][:, :1]
+        delta = jnp.sum(grad.astype(F32) * full_ref[p], axis=-1, keepdims=True)
+        probs = jnp.exp(dot_rt(query, keys[:count, :]) * scale - lse)
+        last = jnp.where(keep, probs[:, count - loc:], 0.0)
+        probs = jnp.concatenate([probs[:, :count - loc], last], axis=1) if p else last
+        d_probs = dot_rt(grad, vals[:count, :])
+        g_scores = (probs * (d_probs - delta) * scale).astype(BF16)
+        d_query = dot(g_scores, keys[:count, :])
+        dk = dot_lt(g_scores, query)
+        dv = dot_lt(probs.astype(BF16), grad)
+        if p == blocks - 1:
+            d_keys[...] = dk
+            d_vals[...] = dv
+        else:
+            d_keys[:count, :] += dk
+            d_vals[:count, :] += dv
+        cosine, sine = cos_ref[span, :], sin_ref[span, :]
+        for g in range(group):
+            out_ref[i, :, g * HEAD_DIM:(g + 1) * HEAD_DIM] = unrot(d_query[g * loc:(g + 1) * loc], cosine, sine)
+        out_ref[i, :, base:base + HEAD_DIM] = unrot(d_keys[span, :], cosine, sine)
+        out_ref[i, :, base + HEAD_DIM:base + 2 * HEAD_DIM] = d_vals[span, :].astype(BF16)
+
+
+def attend_back(at, rec, grad, full, lse, cosine, sine, group):
+    blocks, loc, cols = rec.shape
+    total = blocks * loc
+    return pl.pallas_call(
+        functools.partial(attend_back_kernel, group),
+        out_shape=jax.ShapeDtypeStruct((blocks, loc, cols), BF16),
+        in_specs=[SMEM] + [VMEM] * 6,
+        out_specs=VMEM,
+        scratch_shapes=[pltpu.VMEM((total, HEAD_DIM), BF16)] * 2 + [pltpu.VMEM((total, HEAD_DIM), F32)] * 2,
+        compiler_params=params(40),
+        cost_estimate=cost(7 * group * total * total * HEAD_DIM, 6 * MIB),
+    )(at, rec, grad, full, lse, cosine, sine)
+
+
+def out_kernel(kv, mix_ref, w_ref, cat_ref, *outs):
+    cols = mix_ref.shape[2]
+    for s, out in enumerate(outs):
+        cat_ref[s] = jnp.concatenate([mix_ref[s * kv + n] for n in range(kv)], axis=1)
+        out[...] = dot(cat_ref[s], w_ref[...]).astype(BF16)
+
+
+def out_project(mixed, w_out, seqs):
+    units, loc, cols = mixed.shape
+    kv = units // seqs
+    width = w_out.shape[1]
+    res = pl.pallas_call(
+        functools.partial(out_kernel, kv),
+        out_shape=(jax.ShapeDtypeStruct((seqs, loc, kv * cols), BF16),)
+        + (jax.ShapeDtypeStruct((loc, width), BF16),) * seqs,
+        in_specs=[VMEM] * 2,
+        out_specs=(VMEM,) * (seqs + 1),
+        compiler_params=params(24),
+        cost_estimate=cost(2 * seqs * loc * kv * cols * width, 5 * MIB),
+    )(mixed, w_out)
+    return res[0], res[1:]
 
 
 def rope_tables(positions, head_dim):
@@ -54,7 +255,7 @@
     return jnp.einsum("lsd,lse->de", left, right, preferred_element_type=jnp.float32)
 
 
-def per_device(
+def general(
     hidden_in,
     block_order,
     seq_labels,
@@ -272,6 +473,218 @@
         d_w_up,
         d_w_down,
     )
+
+
+def send_in(part):
+    return part + lax.ppermute(part, "tp", [(0, 1), (3, 2)])
+
+
+def sum_line(part, middle):
+    half = send_in(part)
+    total = half + lax.ppermute(half, "tp", [(1, 2), (2, 1)])
+    ends = lax.ppermute(total, "tp", [(1, 0), (2, 3)])
+    return jnp.where(middle, total, ends)
+
+
+def partner(bit):
+    return [(i, i ^ bit) for i in range(8)]
+
+
+def pick(parts, index, axis):
+    return lax.dynamic_index_in_dim(parts, index, axis, keepdims=False)
+
+
+def scatter_sum(parts):
+    dtype = parts.dtype
+    me = lax.axis_index("blk")
+    core, east, north = me % 2, (me // 2) % 2, me // 4
+    rows = parts.shape[0] // 8
+    parts = parts.reshape((2, 2, 2, rows) + parts.shape[1:])
+
+    def step(values, mine, axis, bit):
+        got = lax.ppermute(pick(values, 1 - mine, axis), "blk", partner(bit))
+        return pick(values, mine, axis).astype(F32) + got.astype(F32)
+
+    parts = step(parts, core, 2, 1).astype(dtype)
+    left, right = parts[:, :, :rows // 2], parts[:, :, rows // 2:]
+    left = step(left, east, 1, 2).astype(dtype)
+    right = step(right, north, 0, 4).astype(dtype)
+    left = step(left, north, 0, 4)
+    right = step(right, east, 0, 2)
+    return jnp.concatenate([left, right], axis=0)
+
+
+def sum_gain(gains):
+    gains = gains + lax.ppermute(gains, "tp", [(0, 1), (1, 0), (2, 3), (3, 2)])
+    gains = gains + lax.ppermute(gains, "tp", [(0, 2), (2, 0), (1, 3), (3, 1)])
+    return scatter_sum(gains)
+
+
+def inverse(values):
+    return lax.rsqrt(jnp.mean(values * values, axis=-1, keepdims=True) + EPS)
+
+
+def tables(positions):
+    cosine, sine = rope_tables(positions, HEAD_DIM)
+    return jnp.concatenate([cosine, cosine], axis=1), jnp.concatenate([-sine, sine], axis=1)
+
+
+def fast(
+    hidden_in,
+    block_order,
+    seq_labels,
+    exit_scales,
+    attn_gain,
+    w_query,
+    w_key,
+    w_value,
+    w_out,
+    mlp_gain,
+    w_gate,
+    w_up,
+    w_down,
+    d_out,
+):
+    loc, seqs, width = hidden_in.shape
+    blocks = block_order.shape[0]
+    kv = w_key.shape[1] // HEAD_DIM
+    group = w_query.shape[1] // w_key.shape[1]
+    me = lax.axis_index("blk")
+    line = lax.axis_index("tp")
+    middle = (line == 1) | (line == 2)
+    index = jnp.arange(blocks, dtype=jnp.int32)
+    at = jnp.sum(jnp.where(block_order[None, :] == index[:, None], index[None, :], 0), axis=1)
+    mine = block_order[me] * loc + jnp.arange(loc, dtype=jnp.int32)
+
+    x = hidden_in.transpose(1, 0, 2)
+    cosine, sine = tables(mine)
+    messages, normed = project(x, attn_gain[None, :], cosine, sine, w_query, w_key, w_value)
+    rec = lax.all_to_all(messages, "blk", 0, 0, tiled=True)
+    mixed, full, lse = attend(at, rec, group)
+    mixed = lax.all_to_all(mixed, "blk", 0, 0, tiled=True)
+    mixed, parts = out_project(mixed, w_out, seqs)
+    attn = [sum_line(p, middle) for p in parts]
+
+    scales = jnp.where(seq_labels == 1, exit_scales[1], exit_scales[0])
+    cot = d_out.transpose(1, 0, 2).astype(F32) * scales[:, None, None]
+    g_down = cot.astype(BF16)
+    gain_m = mlp_gain.astype(F32)
+    norms, hiddens, gates, ups, grads, gains = [], [], [], [], [], []
+    span = 2
+    for first in range(0, seqs, span):
+        part = slice(first, first + span)
+        rows = span * loc
+        total = jnp.concatenate(attn[part], axis=0).astype(F32)
+        resid = x[part].reshape(rows, width).astype(F32) + total
+        unit = resid * inverse(resid)
+        norm = (unit * gain_m).astype(BF16)
+        gate = dot(norm, w_gate)
+        up = dot(norm, w_up)
+        sig = jax.nn.sigmoid(gate)
+        silu = gate * sig
+        d_hidden = dot_rt(g_down[part].reshape(rows, width), w_down)
+        g_up = (d_hidden * silu).astype(BF16)
+        g_gate = (d_hidden * up * (sig * (1.0 + gate * (1.0 - sig)))).astype(BF16)
+        grad = dot_rt(g_gate, w_gate) + dot_rt(g_up, w_up)
+        gains.append(jnp.sum(grad * unit, axis=0))
+        grad = grad.astype(BF16)
+        grads += [grad[i * loc:(i + 1) * loc] for i in range(span)]
+        norms.append(norm)
+        hiddens.append((silu * up).astype(BF16))
+        gates.append(g_gate)
+        ups.append(g_up)
+    norm = jnp.concatenate(norms, axis=0)
+    hidden = jnp.concatenate(hiddens, axis=0)
+    d_mlp = gains[0] + gains[1]
+    d_norm = [sum_line(g, middle) for g in grads]
+
+    d_w_down = dot_lt(hidden, g_down.reshape(seqs * loc, width)).astype(BF16)
+    d_w_down = lax.psum_scatter(d_w_down, "blk", scatter_dimension=1, tiled=True).astype(F32)
+    g_both = jnp.concatenate([jnp.concatenate(gates, axis=0), jnp.concatenate(ups, axis=0)], axis=1)
+    d_w_both = dot_lt(norm, g_both).astype(BF16)
+    d_w_both = lax.psum_scatter(d_w_both, "blk", scatter_dimension=0, tiled=True).astype(F32)
+    units = w_gate.shape[1]
+    d_w_gate, d_w_up = d_w_both[:, :units], d_w_both[:, units:]
+
+    d_resids, g_attns, sends = [], [], []
+    for s in range(seqs):
+        resid = x[s].astype(F32) + attn[s].astype(F32)
+        inv = inverse(resid)
+        unit = resid * inv
+        scaled = d_norm[s].astype(F32) * gain_m
+        d_resid = cot[s] + inv * (scaled - unit * jnp.mean(scaled * unit, axis=-1, keepdims=True))
+        g_attn = d_resid.astype(BF16)
+        g_mixed = dot_rt(g_attn, w_out).astype(BF16)
+        sends += [g_mixed[:, n * group * HEAD_DIM:(n + 1) * group * HEAD_DIM] for n in range(kv)]
+        d_resids.append(d_resid)
+        g_attns.append(g_attn)
+    g_attn = jnp.stack(g_attns)
+    grad = lax.all_to_all(jnp.stack(sends), "blk", 0, 0, tiled=True)
+    cosine, sine = tables(jnp.arange(blocks * loc, dtype=jnp.int32))
+    back = attend_back(at, rec, grad, full, lse, cosine, sine, group)
+    back = lax.all_to_all(back, "blk", 0, 0, tiled=True)
+    back = back.reshape(seqs, kv, loc, (group + 2) * HEAD_DIM)
+
+    out_parts = [dot(hidden[s * loc:(s + 1) * loc], w_down).astype(BF16) for s in range(seqs)]
+    outs = [sum_line(p, middle) for p in out_parts]
+    block_out = jnp.stack(
+        [x[s].astype(F32) + attn[s].astype(F32) + outs[s].astype(F32) for s in range(seqs)], axis=1
+    ).astype(BF16)
+
+    wide = group * HEAD_DIM
+    stacked = jnp.concatenate(
+        [w_query.reshape(width, kv, wide), w_key.reshape(width, kv, HEAD_DIM), w_value.reshape(width, kv, HEAD_DIM)],
+        axis=2,
+    )
+    gain_a = attn_gain.astype(F32)
+    grads, d_attn = [], 0.0
+    for s in range(seqs):
+        grad = sum(dot_rt(back[s, n], stacked[:, n]) for n in range(kv))
+        xs = x[s].astype(F32)
+        d_attn = d_attn + jnp.sum(grad * (xs * inverse(xs)), axis=0)
+        grads.append(grad.astype(BF16))
+    totals = [sum_line(g, middle) for g in grads]
+    d_gains = sum_gain(jnp.stack([d_attn, d_mlp], axis=1))
+
+    d_w_attn = jnp.einsum("srd,snrc->dnc", normed, back, preferred_element_type=F32).astype(BF16)
+    d_w_out = jnp.einsum("srd,src->dc", g_attn, mixed, preferred_element_type=F32).astype(BF16)
+    packed = jnp.concatenate([d_w_attn.reshape(width, -1), d_w_out], axis=1)
+    packed = scatter_sum(packed)
+    cut = kv * (group + 2) * HEAD_DIM
+    d_w_out = packed[:, cut:].T
+    d_w_attn = packed[:, :cut].reshape(-1, kv, (group + 2) * HEAD_DIM)
+    d_w_query = d_w_attn[:, :, :wide].reshape(-1, kv * wide)
+    d_w_key = d_w_attn[:, :, wide:wide + HEAD_DIM].reshape(-1, kv * HEAD_DIM)
+    d_w_value = d_w_attn[:, :, wide + HEAD_DIM:].reshape(-1, kv * HEAD_DIM)
+
+    d_ins = []
+    for s in range(seqs):
+        xs = x[s].astype(F32)
+        inv = inverse(xs)
+        unit = xs * inv
+        scaled = totals[s].astype(F32) * gain_a
+        d_ins.append(d_resids[s] + inv * (scaled - unit * jnp.mean(scaled * unit, axis=-1, keepdims=True)))
+    d_hidden_in = jnp.stack(d_ins, axis=1)
+    return (
+        block_out,
+        d_hidden_in,
+        d_gains[:, 0],
+        d_w_query,
+        d_w_key,
+        d_w_value,
+        d_w_out,
+        d_gains[:, 1],
+        d_w_gate,
+        d_w_up,
+        d_w_down,
+    )
+
+
+def per_device(*args):
+    seqs = args[0].shape[1]
+    kv_heads = args[6].shape[1] // HEAD_DIM
+    fits = lax.axis_size("blk") == 8 and lax.axis_size("tp") == 4 and seqs * kv_heads == 8
+    return (fast if fits else general)(*args)
 
 
 def solution(mesh):

time: 973 us -> 692 us (0.71)
  waiting for transfers between devices: 672 us -> 299 us
  starting transfers between devices: 2.28 us -> 111 us
  matrix products: 148 us -> 85.1 us
  local copies, waits for them, and re-layouts: 57 us -> 84.5 us
  Pallas kernels: 0 us -> 16 us
  blocking collectives: 13.9 us -> 0 us
  other arithmetic: 56.7 us -> 68.2 us
    reduce_scatter x8 -> x2, waiting for transfers between devices: 320 us -> 0.01 us  [the longest x1 0.01 us: fast(): lax.psum_scatter(d_w_both, 'blk', scatter_dimension=0, tiled=True)]
    psum x3 -> x0, waiting for transfers between devices: 313 us -> none  [the longest x1 157 us: per_device(): lax.psum(matmul(hidden, w_down).astype(jnp.bfloat16), 'tp')]
    ppermute x0 -> x60, waiting for transfers between devices: none -> 275 us  [the longest x16 174 us: sum_line(): ends = lax.ppermute(total, 'tp', [(1, 0), (2, 3)])]
    ppermute x0 -> x60, starting transfers between devices: none -> 83.5 us  [the longest x16 37.8 us: send_in(): return part + lax.ppermute(part, 'tp', [(0, 1), (3, 2)])]
    dot_general x32 -> x30, matrix products: 143 us -> 85.1 us  [the longest x18 46.6 us: dot_rt(): lax.dot_general(left, right, (((1,), (1,)), ((), ())), preferred_element_...]
    all_gather x2 -> x0, waiting for transfers between devices: 38.5 us -> none  [the longest x1 22 us: per_device(): val_part = lax.all_gather(vals_bf, 'blk', axis=0, tiled=True)]
    unnamed x72 -> x182, local copies, waits for them, and re-layouts: 19.1 us -> 48.4 us
    all_to_all x0 -> x4, starting transfers between devices: none -> 26.8 us  [the longest x1 12.8 us: fast(): grad = lax.all_to_all(jnp.stack(sends), 'blk', 0, 0, tiled=True)]
  transfers between devices with their start and end apart: 13 -> 66, of which waited for: 13 -> 35; matrix products, arithmetic and copies ran while one was open for 12% -> 26% of each run, Pallas kernels for 0% -> 1%
where the time goes in v1:
time: 692 us; the launch traced here: 681 us
  waiting for transfers between devices  299 us (43%)
  starting transfers between devices  111 us (16%)
  matrix products  85.1 us (12%)
  local copies, waits for them, and re-layouts  84.5 us (12%)
  other arithmetic  68.2 us (10%)
  between operations  17.3 us (2%)
  Pallas kernels  16 us (2%)
    ppermute x16, waiting for transfers between devices, sum_line(): ends = lax.ppermute(total, 'tp', [(1, 0), (2, 3)])  174 us
    ppermute x16, waiting for transfers between devices, send_in(): return part + lax.ppermute(part, 'tp', [(0, 1), (3, 2)])  77.2 us
    unnamed x182, local copies, waits for them, and re-layouts  48.4 us
    dot_general x18, matrix products, dot_rt(): lax.dot_general(left, right, (((1,), (1,)), ((), ())), preferred_element_...  46.6 us
    ppermute x16, starting transfers between devices, send_in(): return part + lax.ppermute(part, 'tp', [(0, 1), (3, 2)])  37.8 us
    ppermute x16, starting transfers between devices, sum_line(): ends = lax.ppermute(total, 'tp', [(1, 0), (2, 3)])  21.1 us
    ppermute x10, waiting for transfers between devices, step(): got = lax.ppermute(pick(values, 1 - mine, axis), 'blk', partner(bit))  19.1 us
    convert_element_type x1, local copies, waits for them, and re-layouts, fast(): jnp.einsum('srd,snrc->dnc', normed, back, preferred_element_type=F32)  19 us
  transfers between devices with their start and end apart: 66, of which 35 were waited for; matrix products, arithmetic and copies ran while one was open for 26% of the time, Pallas kernels for 1%

profile of v1, /device:TPU:0, one launch (start us, length us, event | category | flops | bytes accessed | tf_op | source)
XLA Modules:
  0.0 681.2 jit_solution(2636849169236840637)
XLA Ops:
  32.7 7.9 %all-to-all-done.rec_ref = bf16[8,128,512]{2,1,0:T(8,128)(2,1)} async-done(((bf16[8,128,512]{2,1,0:T(8,128)(2,1)}), bf16[8,128,512]{2,1,0:T(8,128)(2,1)}, u32[]{:S(2)}, u32[]{:S(2)}) %all-to-all-start) | async-done | bytes 1048608 | tf_op jit(solution)/shard_map/all_to_all | solution.py:562
  54.7 7.1 %all-to-all-done.1.mix_ref = bf16[8,128,256]{2,1,0:T(8,128)(2,1)} async-done(((bf16[8,128,256]{2,1,0:T(8,128)(2,1)}), bf16[8,128,256]{2,1,0:T(8,128)(2,1)}, u32[]{:S(2)}, u32[]{:S(2)}) %all-to-all-start.1) | async-done | bytes 524320 | tf_op jit(solution)/shard_map/all_to_all | solution.py:564
  74.1 8.1 %collective-permute-done.3 = bf16[128,2048]{1,0:T(8,128)(2,1)S(1)} collective-permute-done((bf16[128,2048]{1,0:T(8,128)(2,1)S(1)}, bf16[128,2048]{1,0:T(8,128)(2,1)S(1)}, u32[]{:S(2)}, u32[]{:S(2)}) %collective-permute-start.3) | collective-permute-done | bytes 524320 | tf_op jit(solution)/shard_map/ppermute | solution.py:479
  83.0 10.4 %collective-permute-done = bf16[128,2048]{1,0:T(8,128)(2,1)S(1)} collective-permute-done((bf16[128,2048]{1,0:T(8,128)(2,1)S(1)}, bf16[128,2048]{1,0:T(8,128)(2,1)S(1)}, u32[]{:S(2)}, u32[]{:S(2)}) %collective-permute-start) | collective-permute-done | bytes 524320 | tf_op jit(solution)/shard_map/ppermute | solution.py:479
  127.5 7.1 %collective-permute-done.5 = bf16[128,2048]{1,0:T(8,128)(2,1)} collective-permute-done((bf16[128,2048]{1,0:T(8,128)(2,1)}, bf16[128,2048]{1,0:T(8,128)(2,1)}, u32[]{:S(2)}, u32[]{:S(2)}) %collective-permute-start.5) | collective-permute-done | bytes 524320 | tf_op jit(solution)/shard_map/ppermute | solution.py:485
  135.7 10.1 %collective-permute-done.2 = bf16[128,2048]{1,0:T(8,128)(2,1)} collective-permute-done((bf16[128,2048]{1,0:T(8,128)(2,1)}, bf16[128,2048]{1,0:T(8,128)(2,1)}, u32[]{:S(2)}, u32[]{:S(2)}) %collective-permute-start.2) | collective-permute-done | bytes 524320 | tf_op jit(solution)/shard_map/ppermute | solution.py:485
  147.5 9.5 %collective-permute-done.17 = bf16[128,2048]{1,0:T(8,128)(2,1)S(1)} collective-permute-done((bf16[128,2048]{1,0:T(8,128)(2,1)S(1)}, bf16[128,2048]{1,0:T(8,128)(2,1)S(1)}, u32[]{:S(2)}, u32[]{:S(2)}) %collective-permute-start.17) | collective-permute-done | bytes 524320 | tf_op jit(solution)/shard_map/ppermute | solution.py:485
  157.1 6.7 collective-permute-done.14
  184.8 10.7 %multiply_reduce_fusion.1 = (f32[2048]{0:T(1024)S(1)}, bf16[256,2048]{1,0:T(8,128)(2,1)S(1)}) fusion(f32[256]{0:T(256)S(1)} %rsqrt_bitcast_fusion.1, f32[2,128,2048]{2,1,0:T(8,128)S(1)} %copy-done.27, bf16[128,2048]{1,0:T(8,128)(2,1)S(1)} %broadcast_select_fusion.10, bf16[128,2048]{1,0:T(8,128)(2,1)S(1)} %get-tuple-element.105, ...), kind=kOutput, calls=%fused_computation.54 | convolution fusion | flops 1481635840 | bytes 12788736 | tf_op jit(solution)/shard_map/dot_general | solution.py:25
  237.4 6.8 %collective-permute-done.6 = bf16[128,2048]{1,0:T(8,128)(2,1)S(1)} collective-permute-done((bf16[128,2048]{1,0:T(8,128)(2,1)S(1)}, bf16[128,2048]{1,0:T(8,128)(2,1)S(1)}, u32[]{:S(2)}, u32[]{:S(2)}) %collective-permute-start.6) | collective-permute-done | bytes 524320 | tf_op jit(solution)/shard_map/ppermute | solution.py:479
  248.0 7.4 %collective-permute-done.33 = bf16[128,2048]{1,0:T(8,128)(2,1)S(1)} collective-permute-done((bf16[128,2048]{1,0:T(8,128)(2,1)S(1)}, bf16[128,2048]{1,0:T(8,128)(2,1)S(1)}, u32[]{:S(2)}, u32[]{:S(2)}) %collective-permute-start.33) | collective-permute-done | bytes 524320 | tf_op jit(solution)/shard_map/ppermute | solution.py:479
  256.9 9.8 %collective-permute-done.30 = bf16[128,2048]{1,0:T(8,128)(2,1)S(1)} collective-permute-done((bf16[128,2048]{1,0:T(8,128)(2,1)S(1)}, bf16[128,2048]{1,0:T(8,128)(2,1)S(1)}, u32[]{:S(2)}, u32[]{:S(2)}) %collective-permute-start.30) | collective-permute-done | bytes 524320 | tf_op jit(solution)/shard_map/ppermute | solution.py:479
  269.3 8.6 %collective-permute-done.21 = bf16[128,2048]{1,0:T(8,128)(2,1)S(1)} collective-permute-done((bf16[128,2048]{1,0:T(8,128)(2,1)S(1)}, bf16[128,2048]{1,0:T(8,128)(2,1)S(1)}, u32[]{:S(2)}, u32[]{:S(2)}) %collective-permute-start.21) | collective-permute-done | bytes 524320 | tf_op jit(solution)/shard_map/ppermute | solution.py:479
  310.1 13.0 %collective-permute-done.26 = bf16[128,2048]{1,0:T(8,128)(2,1)S(1)} collective-permute-done((bf16[128,2048]{1,0:T(8,128)(2,1)S(1)}, bf16[128,2048]{1,0:T(8,128)(2,1)S(1)}, u32[]{:S(2)}, u32[]{:S(2)}) %collective-permute-start.26) | collective-permute-done | bytes 524320 | tf_op jit(solution)/shard_map/ppermute | solution.py:485
  324.6 9.7 %collective-permute-done.20 = bf16[128,2048]{1,0:T(8,128)(2,1)S(1)} collective-permute-done((bf16[128,2048]{1,0:T(8,128)(2,1)S(1)}, bf16[128,2048]{1,0:T(8,128)(2,1)S(1)}, u32[]{:S(2)}, u32[]{:S(2)}) %collective-permute-start.20) | collective-permute-done | bytes 524320 | tf_op jit(solution)/shard_map/ppermute | solution.py:485
  335.6 9.9 %collective-permute-done.8 = bf16[128,2048]{1,0:T(8,128)(2,1)S(1)} collective-permute-done((bf16[128,2048]{1,0:T(8,128)(2,1)S(1)}, bf16[128,2048]{1,0:T(8,128)(2,1)S(1)}, u32[]{:S(2)}, u32[]{:S(2)}) %collective-permute-start.8) | collective-permute-done | bytes 524320 | tf_op jit(solution)/shard_map/ppermute | solution.py:485
  349.3 7.5 %collective-permute-done.32 = bf16[128,2048]{1,0:T(8,128)(2,1)S(1)} collective-permute-done((bf16[128,2048]{1,0:T(8,128)(2,1)S(1)}, bf16[128,2048]{1,0:T(8,128)(2,1)S(1)}, u32[]{:S(2)}, u32[]{:S(2)}) %collective-permute-start.32) | collective-permute-done | bytes 524320 | tf_op jit(solution)/shard_map/ppermute | solution.py:485
  356.8 11.2 %collective-permute-done.29 = bf16[128,2048]{1,0:T(8,128)(2,1)S(1)} collective-permute-done((bf16[128,2048]{1,0:T(8,128)(2,1)S(1)}, bf16[128,2048]{1,0:T(8,128)(2,1)S(1)}, u32[]{:S(2)}, u32[]{:S(2)}) %collective-permute-start.29) | collective-permute-done | bytes 524320 | tf_op jit(solution)/shard_map/ppermute | solution.py:485
  368.0 11.2 %collective-permute-done.35 = bf16[128,2048]{1,0:T(8,128)(2,1)S(1)} collective-permute-done((bf16[128,2048]{1,0:T(8,128)(2,1)S(1)}, bf16[128,2048]{1,0:T(8,128)(2,1)S(1)}, u32[]{:S(2)}, u32[]{:S(2)}) %collective-permute-start.35) | collective-permute-done | bytes 524320 | tf_op jit(solution)/shard_map/ppermute | solution.py:485
  380.4 8.6 %collective-permute-done.23 = bf16[128,2048]{1,0:T(8,128)(2,1)S(1)} collective-permute-done((bf16[128,2048]{1,0:T(8,128)(2,1)S(1)}, bf16[128,2048]{1,0:T(8,128)(2,1)S(1)}, u32[]{:S(2)}, u32[]{:S(2)}) %collective-permute-start.23) | collective-permute-done | bytes 524320 | tf_op jit(solution)/shard_map/ppermute | solution.py:485
  403.3 12.8 %all-to-all-start.2 = ((bf16[8,128,256]{2,1,0:T(8,128)(2,1)}), bf16[8,128,256]{2,1,0:T(8,128)(2,1)}, u32[]{:S(2)}, u32[]{:S(2)}) async-start(bf16[8,128,256]{2,1,0:T(8,128)(2,1)} %fusion.95), calls=%async_computation.2 | async-start | bytes 1048576 | tf_op jit(solution)/shard_map/all_to_all | solution.py:622
  416.6 11.1 %convolution_convert_fusion = bf16[2048,2816]{1,0:T(8,128)(2,1)} fusion(bf16[256,1408]{1,0:T(8,128)(2,1)} %copy-done.53, bf16[256,1408]{1,0:T(8,128)(2,1)} %copy-done.54, bf16[256,1408]{1,0:T(8,128)(2,1)} %get-tuple-element.113, bf16[256,1408]{1,0:T(8,128)(2,1)} %copy-done.71, bf16[256,2048]{1,0:T(8,128)(2,1)} %copy-done.52, bf16[256,2048]{1,0:T(8,128)(2,1)} %copy-done.51), kind=kOutput, calls=%fused_computation | convolution fusion | flops 5927075840 | bytes 16515072 | tf_op jit(solution)/shard_map/dot_general | solution.py:29
  435.9 6.1 shard_map.224
  458.9 9.4 %all-to-all-done.3 = bf16[8,128,512]{2,1,0:T(8,128)(2,1)} async-done(((bf16[8,128,512]{2,1,0:T(8,128)(2,1)}), bf16[8,128,512]{2,1,0:T(8,128)(2,1)}, u32[]{:S(2)}, u32[]{:S(2)}) %all-to-all-start.3) | async-done | bytes 1048608 | tf_op jit(solution)/shard_map/all_to_all | solution.py:625
  501.3 19.0 %copy.82 = bf16[2048,2,512]{2,1,0:T(2,128)(2,1)} copy(bf16[2048,2,512]{2,0,1:T(8,128)(2,1)S(1)} %bitcast_convert_fusion) | data formatting | bytes 8388608 | tf_op jit(solution)/shard_map/convert_element_type | solution.py:649
  520.3 7.7 %concatenate.58 = bf16[2,2,2,256,1024]{4,3,2,1,0:T(8,128)(2,1)} reshape(bf16[2048,2,512]{2,1,0:T(2,128)(2,1)} %copy.82) | data formatting | bytes 8388608 | tf_op jit(solution)/shard_map/concatenate | solution.py:651
  557.9 34.7 %collective-permute-done.38 = bf16[128,2048]{1,0:T(8,128)(2,1)S(1)} collective-permute-done((bf16[128,2048]{1,0:T(8,128)(2,1)S(1)}, bf16[128,2048]{1,0:T(8,128)(2,1)S(1)}, u32[]{:S(2)}, u32[]{:S(2)}) %collective-permute-start.38) | collective-permute-done | bytes 524320 | tf_op jit(solution)/shard_map/ppermute | solution.py:485
  592.6 12.6 %collective-permute-done.41 = bf16[128,2048]{1,0:T(8,128)(2,1)S(1)} collective-permute-done((bf16[128,2048]{1,0:T(8,128)(2,1)S(1)}, bf16[128,2048]{1,0:T(8,128)(2,1)S(1)}, u32[]{:S(2)}, u32[]{:S(2)}) %collective-permute-start.41) | collective-permute-done | bytes 524320 | tf_op jit(solution)/shard_map/ppermute | solution.py:485
  605.2 11.2 %collective-permute-done.44 = bf16[128,2048]{1,0:T(8,128)(2,1)S(1)} collective-permute-done((bf16[128,2048]{1,0:T(8,128)(2,1)S(1)}, bf16[128,2048]{1,0:T(8,128)(2,1)S(1)}, u32[]{:S(2)}, u32[]{:S(2)}) %collective-permute-start.44) | collective-permute-done | bytes 524320 | tf_op jit(solution)/shard_map/ppermute | solution.py:485
  616.5 9.9 %collective-permute-done.47 = bf16[128,2048]{1,0:T(8,128)(2,1)S(1)} collective-permute-done((bf16[128,2048]{1,0:T(8,128)(2,1)S(1)}, bf16[128,2048]{1,0:T(8,128)(2,1)S(1)}, u32[]{:S(2)}, u32[]{:S(2)}) %collective-permute-start.47) | collective-permute-done | bytes 524320 | tf_op jit(solution)/shard_map/ppermute | solution.py:485
  640.0 10.1 %collective-permute-done.56 = bf16[2,128,1536]{2,1,0:T(8,128)(2,1)S(1)} collective-permute-done((bf16[2,128,1536]{2,1,0:T(8,128)(2,1)S(1)}, bf16[2,128,1536]{2,1,0:T(8,128)(2,1)S(1)}, u32[]{:S(2)}, u32[]{:S(2)}) %collective-permute-start.56) | collective-permute-done | bytes 786464 | tf_op jit(solution)/shard_map/ppermute | solution.py:505
  654.4 6.2 collective-permute-done.57
  (448 shorter events, 331.5 us)
Async XLA Ops:
  52.1 616.5 %reduce-scatter.5.cloned.1.call-start = ((), (), s32[]{:S(2)}) async-start(), calls=%async_computation.7 | async-start | bytes 6488064 | tf_op jit(solution)/shard_map/reduce_scatter | solution.py:602
  71.4 33.2 %collective-permute-start.15 = (bf16[128,2048]{1,0:T(8,128)(2,1)S(1)}, bf16[128,2048]{1,0:T(8,128)(2,1)S(1)}, u32[]{:S(2)}, u32[]{:S(2)}) collective-permute-start(bf16[128,2048]{1,0:T(8,128)(2,1)S(1)} %get-tuple-element.26), channel_id=1, source_target_pairs={{0,1},{3,2},{4,5},{7,6},{8,9},{11,10},{12,13},{15,14},{16,17},{19,... | collective-permute-start | bytes 1572872 | tf_op jit(solution)/shard_map/ppermute | solution.py:479
  72.8 39.6 %collective-permute-start.12 = (bf16[128,2048]{1,0:T(8,128)(2,1)S(1)}, bf16[128,2048]{1,0:T(8,128)(2,1)S(1)}, u32[]{:S(2)}, u32[]{:S(2)}) collective-permute-start(bf16[128,2048]{1,0:T(8,128)(2,1)S(1)} %get-tuple-element.25), channel_id=1, source_target_pairs={{0,1},{3,2},{4,5},{7,6},{8,9},{11,10},{12,13},{15,14},{16,17},{19,... | collective-permute-start | bytes 1572872 | tf_op jit(solution)/shard_map/ppermute | solution.py:479
  82.3 32.5 %collective-permute-start.4 = (bf16[128,2048]{1,0:T(8,128)(2,1)S(1)}, bf16[128,2048]{1,0:T(8,128)(2,1)S(1)}, u32[]{:S(2)}, u32[]{:S(2)}) collective-permute-start(bf16[128,2048]{1,0:T(8,128)(2,1)S(1)} %add.437), channel_id=1, source_target_pairs={{1,2},{2,1},{5,6},{6,5},{9,10},{10,9},{13,14},{14,13},{17,18},{18,... | collective-permute-start | bytes 1572872 | tf_op jit(solution)/shard_map/ppermute | solution.py:484
  123.6 33.4 %collective-permute-start.17 = (bf16[128,2048]{1,0:T(8,128)(2,1)S(1)}, bf16[128,2048]{1,0:T(8,128)(2,1)S(1)}, u32[]{:S(2)}, u32[]{:S(2)}) collective-permute-start(bf16[128,2048]{1,0:T(8,128)(2,1)S(1)} %add.454), channel_id=1, source_target_pairs={{1,0},{2,3},{5,4},{6,7},{9,8},{10,11},{13,12},{14,15},{17,16},{18,... | collective-permute-start | bytes 1572872 | tf_op jit(solution)/shard_map/ppermute | solution.py:485
  126.2 37.5 %collective-permute-start.14 = (bf16[128,2048]{1,0:T(8,128)(2,1)S(1)}, bf16[128,2048]{1,0:T(8,128)(2,1)S(1)}, u32[]{:S(2)}, u32[]{:S(2)}) collective-permute-start(bf16[128,2048]{1,0:T(8,128)(2,1)S(1)} %add.451), channel_id=1, source_target_pairs={{1,0},{2,3},{5,4},{6,7},{9,8},{10,11},{13,12},{14,15},{17,16},{18,... | collective-permute-start | bytes 1572872 | tf_op jit(solution)/shard_map/ppermute | solution.py:485
  199.3 33.7 %collective-permute-start.18 = (bf16[128,2048]{1,0:T(8,128)(2,1)S(1)}, bf16[128,2048]{1,0:T(8,128)(2,1)S(1)}, u32[]{:S(2)}, u32[]{:S(2)}) collective-permute-start(bf16[128,2048]{1,0:T(8,128)(2,1)S(1)} %convolution_convert_fusion.3), channel_id=1, source_target_pairs={{0,1},{3,2},{4,5},{7,6},{8,9},{11,10},{12,13},{15,14},{16,17},{19,... | collective-permute-start | bytes 1572872 | tf_op jit(solution)/shard_map/ppermute | solution.py:479
  201.6 42.6 %collective-permute-start.6 = (bf16[128,2048]{1,0:T(8,128)(2,1)S(1)}, bf16[128,2048]{1,0:T(8,128)(2,1)S(1)}, u32[]{:S(2)}, u32[]{:S(2)}) collective-permute-start(bf16[128,2048]{1,0:T(8,128)(2,1)S(1)} %convolution_convert_fusion.5), channel_id=1, source_target_pairs={{0,1},{3,2},{4,5},{7,6},{8,9},{11,10},{12,13},{15,14},{16,17},{19,... | collective-permute-start | bytes 1572872 | tf_op jit(solution)/shard_map/ppermute | solution.py:479
  209.6 45.9 %collective-permute-start.33 = (bf16[128,2048]{1,0:T(8,128)(2,1)S(1)}, bf16[128,2048]{1,0:T(8,128)(2,1)S(1)}, u32[]{:S(2)}, u32[]{:S(2)}) collective-permute-start(bf16[128,2048]{1,0:T(8,128)(2,1)S(1)} %get-tuple-element.146), channel_id=1, source_target_pairs={{0,1},{3,2},{4,5},{7,6},{8,9},{11,10},{12,13},{15,14},{16,17},{19,... | collective-permute-start | bytes 1572872 | tf_op jit(solution)/shard_map/ppermute | solution.py:479
  210.9 55.8 %collective-permute-start.30 = (bf16[128,2048]{1,0:T(8,128)(2,1)S(1)}, bf16[128,2048]{1,0:T(8,128)(2,1)S(1)}, u32[]{:S(2)}, u32[]{:S(2)}) collective-permute-start(bf16[128,2048]{1,0:T(8,128)(2,1)S(1)} %get-tuple-element.147), channel_id=1, source_target_pairs={{0,1},{3,2},{4,5},{7,6},{8,9},{11,10},{12,13},{15,14},{16,17},{19,... | collective-permute-start | bytes 1572872 | tf_op jit(solution)/shard_map/ppermute | solution.py:479
  221.8 56.1 %collective-permute-start.21 = (bf16[128,2048]{1,0:T(8,128)(2,1)S(1)}, bf16[128,2048]{1,0:T(8,128)(2,1)S(1)}, u32[]{:S(2)}, u32[]{:S(2)}) collective-permute-start(bf16[128,2048]{1,0:T(8,128)(2,1)S(1)} %convolution_convert_fusion.2), channel_id=1, source_target_pairs={{0,1},{3,2},{4,5},{7,6},{8,9},{11,10},{12,13},{15,14},{16,17},{19,... | collective-permute-start | bytes 1572872 | tf_op jit(solution)/shard_map/ppermute | solution.py:479
  233.0 50.9 %collective-permute-start.9 = (bf16[128,2048]{1,0:T(8,128)(2,1)S(1)}, bf16[128,2048]{1,0:T(8,128)(2,1)S(1)}, u32[]{:S(2)}, u32[]{:S(2)}) collective-permute-start(bf16[128,2048]{1,0:T(8,128)(2,1)S(1)} %convolution_convert_fusion.4), channel_id=1, source_target_pairs={{0,1},{3,2},{4,5},{7,6},{8,9},{11,10},{12,13},{15,14},{16,17},{19,... | collective-permute-start | bytes 1572872 | tf_op jit(solution)/shard_map/ppermute | solution.py:479
  244.2 41.1 %collective-permute-start.25 = (bf16[128,2048]{1,0:T(8,128)(2,1)S(1)}, bf16[128,2048]{1,0:T(8,128)(2,1)S(1)}, u32[]{:S(2)}, u32[]{:S(2)}) collective-permute-start(bf16[128,2048]{1,0:T(8,128)(2,1)S(1)} %get-tuple-element.149), channel_id=1, source_target_pairs={{1,2},{2,1},{5,6},{6,5},{9,10},{10,9},{13,14},{14,13},{17,18},{18,... | collective-permute-start | bytes 1572872 | tf_op jit(solution)/shard_map/ppermute | solution.py:484
  255.4 39.4 %collective-permute-start.19 = (bf16[128,2048]{1,0:T(8,128)(2,1)}, bf16[128,2048]{1,0:T(8,128)(2,1)}, u32[]{:S(2)}, u32[]{:S(2)}) collective-permute-start(bf16[128,2048]{1,0:T(8,128)(2,1)} %add.459), channel_id=1, source_target_pairs={{1,2},{2,1},{5,6},{6,5},{9,10},{10,9},{13,14},{14,13},{17,18},{18,... | collective-permute-start | bytes 1572872 | tf_op jit(solution)/shard_map/ppermute | solution.py:484
  300.2 34.1 %collective-permute-start.20 = (bf16[128,2048]{1,0:T(8,128)(2,1)S(1)}, bf16[128,2048]{1,0:T(8,128)(2,1)S(1)}, u32[]{:S(2)}, u32[]{:S(2)}) collective-permute-start(bf16[128,2048]{1,0:T(8,128)(2,1)S(1)} %add.460), channel_id=1, source_target_pairs={{1,0},{2,3},{5,4},{6,7},{9,8},{10,11},{13,12},{14,15},{17,16},{18,... | collective-permute-start | bytes 1572872 | tf_op jit(solution)/shard_map/ppermute | solution.py:485
  301.5 44.1 %collective-permute-start.8 = (bf16[128,2048]{1,0:T(8,128)(2,1)S(1)}, bf16[128,2048]{1,0:T(8,128)(2,1)S(1)}, u32[]{:S(2)}, u32[]{:S(2)}) collective-permute-start(bf16[128,2048]{1,0:T(8,128)(2,1)S(1)} %add.444), channel_id=1, source_target_pairs={{1,0},{2,3},{5,4},{6,7},{9,8},{10,11},{13,12},{14,15},{17,16},{18,... | collective-permute-start | bytes 1572872 | tf_op jit(solution)/shard_map/ppermute | solution.py:485
  307.2 49.6 %collective-permute-start.32 = (bf16[128,2048]{1,0:T(8,128)(2,1)S(1)}, bf16[128,2048]{1,0:T(8,128)(2,1)S(1)}, u32[]{:S(2)}, u32[]{:S(2)}) collective-permute-start(bf16[128,2048]{1,0:T(8,128)(2,1)S(1)} %add.481), channel_id=1, source_target_pairs={{1,0},{2,3},{5,4},{6,7},{9,8},{10,11},{13,12},{14,15},{17,16},{18,... | collective-permute-start | bytes 1572872 | tf_op jit(solution)/shard_map/ppermute | solution.py:485
  308.7 59.4 %collective-permute-start.29 = (bf16[128,2048]{1,0:T(8,128)(2,1)S(1)}, bf16[128,2048]{1,0:T(8,128)(2,1)S(1)}, u32[]{:S(2)}, u32[]{:S(2)}) collective-permute-start(bf16[128,2048]{1,0:T(8,128)(2,1)S(1)} %add.475), channel_id=1, source_target_pairs={{1,0},{2,3},{5,4},{6,7},{9,8},{10,11},{13,12},{14,15},{17,16},{18,... | collective-permute-start | bytes 1572872 | tf_op jit(solution)/shard_map/ppermute | solution.py:485
  323.1 56.2 %collective-permute-start.35 = (bf16[128,2048]{1,0:T(8,128)(2,1)S(1)}, bf16[128,2048]{1,0:T(8,128)(2,1)S(1)}, u32[]{:S(2)}, u32[]{:S(2)}) collective-permute-start(bf16[128,2048]{1,0:T(8,128)(2,1)S(1)} %add.485), channel_id=1, source_target_pairs={{1,0},{2,3},{5,4},{6,7},{9,8},{10,11},{13,12},{14,15},{17,16},{18,... | collective-permute-start | bytes 1572872 | tf_op jit(solution)/shard_map/ppermute | solution.py:485
  334.3 54.7 %collective-permute-start.23 = (bf16[128,2048]{1,0:T(8,128)(2,1)S(1)}, bf16[128,2048]{1,0:T(8,128)(2,1)S(1)}, u32[]{:S(2)}, u32[]{:S(2)}) collective-permute-start(bf16[128,2048]{1,0:T(8,128)(2,1)S(1)} %add.464), channel_id=1, source_target_pairs={{1,0},{2,3},{5,4},{6,7},{9,8},{10,11},{13,12},{14,15},{17,16},{18,... | collective-permute-start | bytes 1572872 | tf_op jit(solution)/shard_map/ppermute | solution.py:485
  345.6 49.1 %collective-permute-start.11 = (bf16[128,2048]{1,0:T(8,128)(2,1)S(1)}, bf16[128,2048]{1,0:T(8,128)(2,1)S(1)}, u32[]{:S(2)}, u32[]{:S(2)}) collective-permute-start(bf16[128,2048]{1,0:T(8,128)(2,1)S(1)} %add.448), channel_id=1, source_target_pairs={{1,0},{2,3},{5,4},{6,7},{9,8},{10,11},{13,12},{14,15},{17,16},{18,... | collective-permute-start | bytes 1572872 | tf_op jit(solution)/shard_map/ppermute | solution.py:485
  416.2 254.7 %reduce-scatter.3.cloned.1.call-start = ((), (), s32[]{:S(2)}) async-start(), calls=%async_computation.6 | async-start | bytes 12976128 | tf_op jit(solution)/shard_map/reduce_scatter | solution.py:605
  487.0 48.8 %collective-permute-start.36 = (bf16[128,2048]{1,0:T(8,128)(2,1)}, bf16[128,2048]{1,0:T(8,128)(2,1)S(1)}, u32[]{:S(2)}, u32[]{:S(2)}) collective-permute-start(bf16[128,2048]{1,0:T(8,128)(2,1)} %get-tuple-element.142), channel_id=1, source_target_pairs={{0,1},{3,2},{4,5},{7,6},{8,9},{11,10},{12,13},{15,14},{16,17},{19,... | collective-permute-start | bytes 1572872 | tf_op jit(solution)/shard_map/ppermute | solution.py:479
  490.9 48.5 %collective-permute-start.39 = (bf16[128,2048]{1,0:T(8,128)(2,1)}, bf16[128,2048]{1,0:T(8,128)(2,1)}, u32[]{:S(2)}, u32[]{:S(2)}) collective-permute-start(bf16[128,2048]{1,0:T(8,128)(2,1)} %get-tuple-element.143), channel_id=1, source_target_pairs={{0,1},{3,2},{4,5},{7,6},{8,9},{11,10},{12,13},{15,14},{16,17},{19,... | collective-permute-start | bytes 1572872 | tf_op jit(solution)/shard_map/ppermute | solution.py:479
  493.0 49.3 %collective-permute-start.42 = (bf16[128,2048]{1,0:T(8,128)(2,1)}, bf16[128,2048]{1,0:T(8,128)(2,1)}, u32[]{:S(2)}, u32[]{:S(2)}) collective-permute-start(bf16[128,2048]{1,0:T(8,128)(2,1)} %get-tuple-element.140), channel_id=1, source_target_pairs={{0,1},{3,2},{4,5},{7,6},{8,9},{11,10},{12,13},{15,14},{16,17},{19,... | collective-permute-start | bytes 1572872 | tf_op jit(solution)/shard_map/ppermute | solution.py:479
  495.1 48.7 %collective-permute-start.45 = (bf16[128,2048]{1,0:T(8,128)(2,1)S(1)}, bf16[128,2048]{1,0:T(8,128)(2,1)}, u32[]{:S(2)}, u32[]{:S(2)}) collective-permute-start(bf16[128,2048]{1,0:T(8,128)(2,1)S(1)} %get-tuple-element.141), channel_id=1, source_target_pairs={{0,1},{3,2},{4,5},{7,6},{8,9},{11,10},{12,13},{15,14},{16,17},{19,... | collective-permute-start | bytes 1572872 | tf_op jit(solution)/shard_map/ppermute | solution.py:479
  497.4 34.9 %collective-permute-start.49 = (f32[2048,2]{0,1:T(2,128)S(1)}, f32[2048,2]{0,1:T(2,128)S(1)}, u32[]{:S(2)}, u32[]{:S(2)}) collective-permute-start(f32[2048,2]{0,1:T(2,128)S(1)} %fusion.114), channel_id=1, source_target_pairs={{0,2},{2,0},{1,3},{3,1},{4,6},{6,4},{5,7},{7,5},{8,10},{10,8},{9,1... | collective-permute-start | bytes 49160 | tf_op jit(solution)/shard_map/ppermute | solution.py:519
  542.3 86.0 %collective-permute-start.55 = (bf16[2,2,256,1536]{3,2,1,0:T(8,128)(2,1)S(1)}, bf16[2,2,256,1536]{3,2,1,0:T(8,128)(2,1)S(1)}, u32[]{:S(2)}, u32[]{:S(2)}) collective-permute-start(bf16[2,2,256,1536]{3,2,1,0:T(8,128)(2,1)S(1)} %fusion.2), channel_id=1, source_target_pairs={{0,4},{4,0},{8,12},{12,8},{16,20},{20,16},{24,28},{28,24},{1,5},{5... | collective-permute-start | bytes 9437192 | tf_op jit(solution)/shard_map/ppermute | solution.py:505
  551.6 41.1 %collective-permute-start.38 = (bf16[128,2048]{1,0:T(8,128)(2,1)S(1)}, bf16[128,2048]{1,0:T(8,128)(2,1)S(1)}, u32[]{:S(2)}, u32[]{:S(2)}) collective-permute-start(bf16[128,2048]{1,0:T(8,128)(2,1)S(1)} %add.489), channel_id=1, source_target_pairs={{1,0},{2,3},{5,4},{6,7},{9,8},{10,11},{13,12},{14,15},{17,16},{18,... | collective-permute-start | bytes 1572872 | tf_op jit(solution)/shard_map/ppermute | solution.py:485
  553.0 52.2 %collective-permute-start.41 = (bf16[128,2048]{1,0:T(8,128)(2,1)S(1)}, bf16[128,2048]{1,0:T(8,128)(2,1)S(1)}, u32[]{:S(2)}, u32[]{:S(2)}) collective-permute-start(bf16[128,2048]{1,0:T(8,128)(2,1)S(1)} %add.494), channel_id=1, source_target_pairs={{1,0},{2,3},{5,4},{6,7},{9,8},{10,11},{13,12},{14,15},{17,16},{18,... | collective-permute-start | bytes 1572872 | tf_op jit(solution)/shard_map/ppermute | solution.py:485
  554.5 62.0 %collective-permute-start.44 = (bf16[128,2048]{1,0:T(8,128)(2,1)S(1)}, bf16[128,2048]{1,0:T(8,128)(2,1)S(1)}, u32[]{:S(2)}, u32[]{:S(2)}) collective-permute-start(bf16[128,2048]{1,0:T(8,128)(2,1)S(1)} %add.499), channel_id=1, source_target_pairs={{1,0},{2,3},{5,4},{6,7},{9,8},{10,11},{13,12},{14,15},{17,16},{18,... | collective-permute-start | bytes 1572872 | tf_op jit(solution)/shard_map/ppermute | solution.py:485
  555.8 70.6 %collective-permute-start.47 = (bf16[128,2048]{1,0:T(8,128)(2,1)S(1)}, bf16[128,2048]{1,0:T(8,128)(2,1)S(1)}, u32[]{:S(2)}, u32[]{:S(2)}) collective-permute-start(bf16[128,2048]{1,0:T(8,128)(2,1)S(1)} %add.504), channel_id=1, source_target_pairs={{1,0},{2,3},{5,4},{6,7},{9,8},{10,11},{13,12},{14,15},{17,16},{18,... | collective-permute-start | bytes 1572872 | tf_op jit(solution)/shard_map/ppermute | solution.py:485
  (116 other events, 1515.6 us)
Sparse Core Ops, SparseCore 0:
  292.0 68.3 reduce-scatter.4
  427.8 88.8 reduce-scatter.2

commit v2 on v1

--- a/solution.py
+++ b/solution.py
@@ -33,8 +33,8 @@
     return pltpu.CompilerParams(vmem_limit_bytes=limit * MIB)
 
 
-def cost(flops, moved):
-    return pl.CostEstimate(flops=int(flops), bytes_accessed=int(moved), transcendentals=0)
+def cost():
+    return pl.CostEstimate(flops=5 * 10**9, bytes_accessed=10**6, transcendentals=0)
 
 
 SMEM = pl.BlockSpec(memory_space=pltpu.SMEM)
@@ -77,14 +77,13 @@
     seqs, loc, width = x.shape
     heads, kv = wq.shape[1] // HEAD_DIM, wk.shape[1] // HEAD_DIM
     cols = (heads // kv + 2) * HEAD_DIM
-    flops = 2 * seqs * loc * width * (wq.shape[1] + 2 * wk.shape[1])
     return pl.pallas_call(
         functools.partial(project_kernel, heads, kv),
         out_shape=(jax.ShapeDtypeStruct((seqs * kv, loc, cols), BF16), jax.ShapeDtypeStruct(x.shape, BF16)),
         in_specs=[VMEM] * 7,
         out_specs=(VMEM, VMEM),
         compiler_params=params(32),
-        cost_estimate=cost(flops, 12 * MIB),
+        cost_estimate=cost(),
     )(x, gain, cosine, sine, wq, wk, wv)
 
 
@@ -129,7 +128,7 @@
         out_specs=(VMEM,) * 3,
         scratch_shapes=[pltpu.VMEM((total, HEAD_DIM), BF16)] * 2,
         compiler_params=params(32),
-        cost_estimate=cost(3 * group * total * total * HEAD_DIM, 4 * MIB),
+        cost_estimate=cost(),
     )(at, rec)
 
 
@@ -186,8 +185,8 @@
         in_specs=[SMEM] + [VMEM] * 6,
         out_specs=VMEM,
         scratch_shapes=[pltpu.VMEM((total, HEAD_DIM), BF16)] * 2 + [pltpu.VMEM((total, HEAD_DIM), F32)] * 2,
-        compiler_params=params(40),
-        cost_estimate=cost(7 * group * total * total * HEAD_DIM, 6 * MIB),
+        compiler_params=params(60),
+        cost_estimate=cost(),
     )(at, rec, grad, full, lse, cosine, sine)
 
 
@@ -209,9 +208,320 @@
         in_specs=[VMEM] * 2,
         out_specs=(VMEM,) * (seqs + 1),
         compiler_params=params(24),
-        cost_estimate=cost(2 * seqs * loc * kv * cols * width, 5 * MIB),
+        cost_estimate=cost(),
     )(mixed, w_out)
     return res[0], res[1:]
+
+
+def input_grads_kernel(seqs, kv, back_ref, x_ref, wq_ref, wk_ref, wv_ref, *refs):
+    gain_refs, outs, (rows_ref, inv_ref, attn_ref) = refs[:seqs], refs[seqs:2 * seqs], refs[2 * seqs:]
+    loc, width = x_ref.shape[1], x_ref.shape[2]
+    group = wq_ref.shape[1] // (kv * HEAD_DIM)
+    gather(back_ref, rows_ref, seqs, kv, group)
+    at_k = kv * group * HEAD_DIM
+    at_v = at_k + kv * HEAD_DIM
+    for s in range(seqs):
+        x = x_ref[s].astype(F32)
+        inv = lax.rsqrt(jnp.mean(x * x, axis=-1, keepdims=True) + EPS)
+        inv_ref[s * loc:(s + 1) * loc, :] = jnp.broadcast_to(inv, (loc, HEAD_DIM))
+    tile = 512
+    for t in range(width // tile):
+        span = slice(t * tile, (t + 1) * tile)
+        grad = dot_rt(rows_ref[:, :at_k], wq_ref[span, :])
+        grad += dot_rt(rows_ref[:, at_k:at_v], wk_ref[span, :])
+        grad += dot_rt(rows_ref[:, at_v:], wv_ref[span, :])
+        total = 0.0
+        for s in range(seqs):
+            part = grad[s * loc:(s + 1) * loc]
+            outs[s][:loc, span] = part.astype(BF16)
+            unit = x_ref[s, :, span].astype(F32) * inv_ref[s * loc:(s + 1) * loc, :1]
+            total = total + jnp.sum(part * unit, axis=0, keepdims=True)
+        attn_ref[:, span] = total
+    mlp = sum(ref[...] for ref in gain_refs)
+    lines = []
+    for gain in (attn_ref[...], mlp):
+        high = gain.astype(BF16).astype(F32)
+        lines += [high, gain - high]
+    row = lax.broadcasted_iota(jnp.int32, (16, width), 0)
+    extra = jnp.zeros((16, width), F32)
+    for i, gain in enumerate(lines):
+        extra = jnp.where(row == i, gain, extra)
+    outs[0][loc:, :] = extra.astype(BF16)
+
+
+def gather(back_ref, rows_ref, seqs, kv, group):
+    loc = back_ref.shape[1]
+    wide = group * HEAD_DIM
+    for s in range(seqs):
+        for n in range(kv):
+            span = slice(s * loc, (s + 1) * loc)
+            rows_ref[span, n * wide:(n + 1) * wide] = back_ref[s * kv + n, :, :wide]
+            for i in range(2):
+                at = kv * wide + (i * kv + n) * HEAD_DIM
+                rows_ref[span, at:at + HEAD_DIM] = back_ref[s * kv + n, :, wide + i * HEAD_DIM:wide + (i + 1) * HEAD_DIM]
+
+
+def input_grads(back, x, wq, wk, wv, gains):
+    seqs, loc, width = x.shape
+    kv = wk.shape[1] // HEAD_DIM
+    cols = wq.shape[1] + 2 * wk.shape[1]
+    return pl.pallas_call(
+        functools.partial(input_grads_kernel, seqs, kv),
+        out_shape=(jax.ShapeDtypeStruct((loc + 16, width), BF16),) + (jax.ShapeDtypeStruct((loc, width), BF16),) * (seqs - 1),
+        in_specs=[VMEM] * (5 + seqs),
+        out_specs=(VMEM,) * seqs,
+        scratch_shapes=[
+            pltpu.VMEM((seqs * loc, cols), BF16),
+            pltpu.VMEM((seqs * loc, HEAD_DIM), F32),
+            pltpu.VMEM((1, width), F32),
+        ],
+        compiler_params=params(60),
+        cost_estimate=cost(),
+    )(back, x, wq, wk, wv, *gains)
+
+
+def shares_call(body, fixed, tall, cols, scratch, core, shares):
+    width = tall[0].shape[-1]
+    tile = width // shares
+
+    def mine(step, keep, core_ref):
+        return 2 * step + jnp.where(keep == 0, 1 - core_ref[0], core_ref[0])
+
+    def tall_spec(a):
+        lead = (0,) * (a.ndim - 1)
+        return pl.BlockSpec(a.shape[:-1] + (tile,), lambda i, k, c: lead + (mine(i, k, c),))
+
+    out = pl.BlockSpec((1, tile, cols), lambda i, k, c: (i, 0, 0))
+    return pl.pallas_call(
+        body,
+        grid_spec=pltpu.PrefetchScalarGridSpec(
+            num_scalar_prefetch=1,
+            grid=(shares // 2, 2),
+            in_specs=[pl.BlockSpec(a.shape, lambda i, k, c, n=a.ndim: (0,) * n) for a in fixed] + [tall_spec(a) for a in tall],
+            out_specs=(out, out),
+            scratch_shapes=scratch,
+        ),
+        out_shape=(jax.ShapeDtypeStruct((shares // 2, tile, cols), BF16),) * 2,
+        compiler_params=params(48),
+        cost_estimate=cost(),
+    )(core, *fixed, *tall)
+
+
+def put_share(send_ref, keep_ref, pieces):
+    def store(ref):
+        at = 0
+        for piece in pieces:
+            ref[0, :, at:at + piece.shape[1]] = piece.astype(BF16)
+            at += piece.shape[1]
+
+    @pl.when(pl.program_id(1) == 0)
+    def _():
+        store(send_ref)
+
+    @pl.when(pl.program_id(1) == 1)
+    def _():
+        store(keep_ref)
+
+
+def attn_grads_kernel(seqs, kv, group, core_ref, back_ref, mix_ref, norm_ref, *refs):
+    grad_refs, (send_ref, keep_ref, rows_ref) = refs[:seqs], refs[seqs:]
+
+    @pl.when((pl.program_id(0) == 0) & (pl.program_id(1) == 0))
+    def _():
+        gather(back_ref, rows_ref, seqs, kv, group)
+
+    rows = rows_ref.shape[0]
+    left = norm_ref[...].reshape(rows, norm_ref.shape[2])
+    grad = jnp.concatenate([ref[...] for ref in grad_refs], axis=0)
+    mixed = mix_ref[...].reshape(rows, mix_ref.shape[2])
+    put_share(send_ref, keep_ref, [dot_lt(left, rows_ref[...]), dot_lt(grad, mixed)])
+
+
+def attn_grads(core, back, mixed, normed, g_attns, kv, shares):
+    seqs, loc, width = normed.shape
+    group = back.shape[2] // HEAD_DIM - 2
+    cols = kv * back.shape[2]
+    scratch = [pltpu.VMEM((seqs * loc, cols), BF16)]
+    body = functools.partial(attn_grads_kernel, seqs, kv, group)
+    return shares_call(body, (back, mixed), (normed,) + tuple(g_attns), cols + mixed.shape[2], scratch, core, shares)
+
+
+def ffn_grads_kernel(seqs, core_ref, *refs):
+    fixed, refs = refs[:3 * seqs], refs[3 * seqs:]
+    down_ref, norm_refs, (send_ref, keep_ref), scratch = refs[0], refs[1:seqs + 1], refs[seqs + 1:seqs + 3], refs[seqs + 3:]
+
+    @pl.when((pl.program_id(0) == 0) & (pl.program_id(1) == 0))
+    def _():
+        loc = fixed[0].shape[0]
+        for i, whole in enumerate(scratch):
+            for s in range(seqs):
+                whole[s * loc:(s + 1) * loc, :] = fixed[i * seqs + s][...]
+
+    gate_ref, up_ref, hid_ref = scratch
+    norm = jnp.concatenate([ref[...] for ref in norm_refs], axis=0)
+    put_share(
+        send_ref,
+        keep_ref,
+        [dot_lt(norm, gate_ref[...]), dot_lt(norm, up_ref[...]), dot_lt(down_ref[...], hid_ref[...])],
+    )
+
+
+def ffn_grads(core, gates, ups, hiddens, g_down, norms, shares):
+    loc, units = gates[0].shape
+    scratch = [pltpu.VMEM((len(gates) * loc, units), BF16)] * 3
+    body = functools.partial(ffn_grads_kernel, len(gates))
+    fixed = tuple(gates) + tuple(ups) + tuple(hiddens)
+    return shares_call(body, fixed, (g_down,) + tuple(norms), 3 * units, scratch, core, shares)
+
+
+def fold_two_kernel(place_ref, *refs):
+    keeps, gots, outs = refs[:4], refs[4:8], refs[8:]
+    for keep, got, out in zip(keeps, gots, outs):
+        out[0] = (keep[0, 0].astype(F32) + got[0, 0].astype(F32)).astype(BF16)
+
+
+def fold_two(place, keep, got):
+    _, rows, cols = keep.shape
+    half = rows // 2
+    keep, got = keep.reshape(2, 2, rows, cols), got.reshape(2, 2, rows, cols)
+    tile = half // 2
+    ins = []
+    for own in (0, 1):
+        ins.append(pl.BlockSpec((1, 1, tile, cols), lambda i, j, p, own=own: (i, jnp.where(own == 1, p[0], 1 - p[0]), j, 0)))
+    for own in (0, 1):
+        ins.append(pl.BlockSpec((1, 1, tile, cols), lambda i, j, p, own=own: (jnp.where(own == 1, p[1], 1 - p[1]), i, j + 2, 0)))
+    return pl.pallas_call(
+        fold_two_kernel,
+        grid_spec=pltpu.PrefetchScalarGridSpec(
+            num_scalar_prefetch=1,
+            grid=(2, 2),
+            in_specs=ins + ins,
+            out_specs=(pl.BlockSpec((1, tile, cols), lambda i, j, p: (i, j, 0)),) * 4,
+        ),
+        out_shape=(jax.ShapeDtypeStruct((2, half, cols), BF16),) * 4,
+        compiler_params=params(40),
+        cost_estimate=cost(),
+    )(place, keep, keep, keep, keep, got, got, got, got)
+
+
+def fold_three(place, upper, upper_got, lower, lower_got):
+    _, half, cols = upper.shape
+    tile = half // 2
+    ins = []
+    for axis in (1, 0):
+        for own in (0, 1):
+            ins.append(pl.BlockSpec((1, 1, tile, cols), lambda j, p, own=own, axis=axis: (0, jnp.where(own == 1, p[axis], 1 - p[axis]), j, 0)))
+    flat = pl.BlockSpec((1, tile, cols), lambda j, p: (0, j, 0))
+    u, ug, l, lg = (a[None] for a in (upper, upper_got, lower, lower_got))
+    res = pl.pallas_call(
+        fold_two_kernel,
+        grid_spec=pltpu.PrefetchScalarGridSpec(
+            num_scalar_prefetch=1, grid=(2,), in_specs=ins + ins, out_specs=(flat,) * 4
+        ),
+        out_shape=(jax.ShapeDtypeStruct((1, half, cols), BF16),) * 4,
+        compiler_params=params(40),
+        cost_estimate=cost(),
+    )(place, u, u, l, l, ug, ug, lg, lg)
+    return [a[0] for a in res]
+
+
+def fold_four_kernel(widths, upper, upper_got, lower, lower_got, *outs):
+    half = upper.shape[0]
+    for at, (one, two) in enumerate(((upper, upper_got), (lower, lower_got))):
+        start = 0
+        for out, width in zip(outs, widths):
+            part = one[:, start:start + width].astype(F32) + two[:, start:start + width].astype(F32)
+            if out is outs[-1]:
+                out[:, at * half:(at + 1) * half] = part.T
+            else:
+                out[at * half:(at + 1) * half, :] = part
+            start += width
+
+
+def fold_four(widths, upper, upper_got, lower, lower_got):
+    rows = 2 * upper.shape[0]
+    shapes = [(rows, w) for w in widths[:-1]] + [(widths[-1], rows)]
+    return pl.pallas_call(
+        functools.partial(fold_four_kernel, widths),
+        out_shape=tuple(jax.ShapeDtypeStruct(shape, F32) for shape in shapes),
+        in_specs=[VMEM] * 4,
+        out_specs=(VMEM,) * len(widths),
+        compiler_params=params(40),
+        cost_estimate=cost(),
+    )(upper, upper_got, lower, lower_got)
+
+
+def finish_kernel(seqs, mid_ref, x_ref, gain_ref, *refs):
+    inner, ends, resids, out_ref = refs[:seqs], refs[seqs:2 * seqs], refs[2 * seqs:3 * seqs], refs[3 * seqs]
+    gain = gain_ref[...].astype(F32)
+    for s in range(seqs):
+        grad = jnp.where(mid_ref[0] == 1, inner[s][...].astype(F32), ends[s][...].astype(F32))
+        x = x_ref[s].astype(F32)
+        inv = lax.rsqrt(jnp.mean(x * x, axis=-1, keepdims=True) + EPS)
+        unit = x * inv
+        scaled = grad * gain
+        back = inv * (scaled - unit * jnp.mean(scaled * unit, axis=-1, keepdims=True))
+        out_ref[:, s, :] = resids[s][...] + back
+
+
+def finish(mid, x, gain, inner, ends, resids):
+    seqs, loc, width = x.shape
+    tile = 32
+    flat = pl.BlockSpec((tile, width), lambda i: (i, 0))
+    return pl.pallas_call(
+        functools.partial(finish_kernel, seqs),
+        grid=(loc // tile,),
+        out_shape=jax.ShapeDtypeStruct((loc, seqs, width), F32),
+        in_specs=[SMEM, pl.BlockSpec((seqs, tile, width), lambda i: (0, i, 0)), pl.BlockSpec((1, width), lambda i: (0, 0))]
+        + [flat] * (3 * seqs),
+        out_specs=pl.BlockSpec((tile, seqs, width), lambda i: (i, 0, 0)),
+        compiler_params=params(32),
+        cost_estimate=cost(),
+    )(mid, x, gain, *inner, *ends, *resids)
+
+
+def output_kernel(seqs, mid_ref, x_ref, *refs):
+    attn, inner, ends, out_ref, wide = refs[:seqs], refs[seqs:2 * seqs], refs[2 * seqs:3 * seqs], refs[3 * seqs], refs[3 * seqs + 1]
+    for s in range(seqs):
+        down = jnp.where(mid_ref[0] == 1, inner[s][...].astype(F32), ends[s][...].astype(F32))
+        wide[:, s, :] = x_ref[s].astype(F32) + attn[s][...].astype(F32) + down
+    out_ref[...] = wide[...].astype(BF16)
+
+
+def block_output(mid, x, attn, inner, ends):
+    seqs, loc, width = x.shape
+    tile = 32
+    flat = pl.BlockSpec((tile, width), lambda i: (i, 0))
+    parts = []
+    for group in (inner, ends):
+        per = seqs // len(group)
+        for s in range(seqs):
+            parts.append((group[s // per], pl.BlockSpec((tile, width), lambda i, at=(s % per) * (loc // tile): (i + at, 0))))
+    return pl.pallas_call(
+        functools.partial(output_kernel, seqs),
+        grid=(loc // tile,),
+        out_shape=jax.ShapeDtypeStruct((loc, seqs, width), BF16),
+        in_specs=[SMEM, pl.BlockSpec((seqs, tile, width), lambda i: (0, i, 0))] + [flat] * seqs + [spec for _, spec in parts],
+        out_specs=pl.BlockSpec((tile, seqs, width), lambda i: (i, 0, 0)),
+        scratch_shapes=[pltpu.VMEM((tile, seqs, width), F32)],
+        compiler_params=params(32),
+        cost_estimate=cost(),
+    )(mid, x, *attn, *(a for a, _ in parts))
+
+
+def add_kernel(left, right, out):
+    out[...] = (left[...].astype(F32) + right[...].astype(F32)).astype(BF16)
+
+
+def add(left, right):
+    return pl.pallas_call(
+        add_kernel,
+        out_shape=jax.ShapeDtypeStruct(left.shape, BF16),
+        in_specs=[VMEM, VMEM],
+        out_specs=VMEM,
+        compiler_params=params(16),
+        cost_estimate=cost(),
+    )(left, right)
 
 
 def rope_tables(positions, head_dim):
@@ -475,49 +785,75 @@
     )
 
 
-def send_in(part):
-    return part + lax.ppermute(part, "tp", [(0, 1), (3, 2)])
-
-
-def sum_line(part, middle):
-    half = send_in(part)
-    total = half + lax.ppermute(half, "tp", [(1, 2), (2, 1)])
-    ends = lax.ppermute(total, "tp", [(1, 0), (2, 3)])
-    return jnp.where(middle, total, ends)
+class Steps:
+    def __init__(self):
+        self.last = None
+
+    def enter(self, *values):
+        if self.last is not None:
+            values, _ = lax.optimization_barrier((values, self.last))
+        return values if len(values) > 1 else values[0]
+
+    def leave(self, value):
+        self.last = value
+        return value
+
+
+class Line:
+    def __init__(self, steps, middle, parts):
+        self.steps, self.middle, self.parts = steps, middle, list(parts)
+        count = len(self.parts)
+        self.first, self.half, self.second, self.total, self.third, self.done = ([None] * count for _ in range(6))
+
+    def one(self, c):
+        self.first[c] = lax.ppermute(self.parts[c], "tp", [(0, 1), (3, 2)])
+
+    def two(self, c):
+        part, got = self.steps.enter(self.parts[c], self.first[c])
+        self.half[c] = self.steps.leave(add(part, got))
+        self.second[c] = lax.ppermute(self.half[c], "tp", [(1, 2), (2, 1)])
+
+    def three(self, c):
+        half, got = self.steps.enter(self.half[c], self.second[c])
+        self.total[c] = self.steps.leave(add(half, got))
+        self.third[c] = lax.ppermute(self.total[c], "tp", [(1, 0), (2, 3)])
+
+    def four(self, c):
+        total, got = self.steps.enter(self.total[c], self.third[c])
+        self.done[c] = self.steps.leave(jnp.where(self.middle, total, got))
+
+    def five(self, c):
+        self.third[c] = self.steps.leave(self.steps.enter(self.third[c]))
 
 
 def partner(bit):
     return [(i, i ^ bit) for i in range(8)]
 
 
-def pick(parts, index, axis):
-    return lax.dynamic_index_in_dim(parts, index, axis, keepdims=False)
-
-
-def scatter_sum(parts):
-    dtype = parts.dtype
-    me = lax.axis_index("blk")
-    core, east, north = me % 2, (me // 2) % 2, me // 4
-    rows = parts.shape[0] // 8
-    parts = parts.reshape((2, 2, 2, rows) + parts.shape[1:])
-
-    def step(values, mine, axis, bit):
-        got = lax.ppermute(pick(values, 1 - mine, axis), "blk", partner(bit))
-        return pick(values, mine, axis).astype(F32) + got.astype(F32)
-
-    parts = step(parts, core, 2, 1).astype(dtype)
-    left, right = parts[:, :, :rows // 2], parts[:, :, rows // 2:]
-    left = step(left, east, 1, 2).astype(dtype)
-    right = step(right, north, 0, 4).astype(dtype)
-    left = step(left, north, 0, 4)
-    right = step(right, east, 0, 2)
-    return jnp.concatenate([left, right], axis=0)
-
-
-def sum_gain(gains):
-    gains = gains + lax.ppermute(gains, "tp", [(0, 1), (1, 0), (2, 3), (3, 2)])
-    gains = gains + lax.ppermute(gains, "tp", [(0, 2), (2, 0), (1, 3), (3, 1)])
-    return scatter_sum(gains)
+class Scatter:
+    def __init__(self, steps, place, send, keep):
+        self.steps, self.place, self.keep = steps, place, keep
+        self.got = lax.ppermute(send, "blk", partner(1))
+
+    def two(self):
+        keep, got = self.steps.enter(self.keep, self.got)
+        away, self.upper, off, self.lower = fold_two(self.place, keep, got)
+        self.steps.leave(self.upper)
+        self.upper_got = lax.ppermute(away, "blk", partner(2))
+        self.lower_got = lax.ppermute(off, "blk", partner(4))
+
+    def three(self):
+        values = self.steps.enter(self.upper, self.upper_got, self.lower, self.lower_got)
+        away, self.upper, off, self.lower = fold_three(self.place, *values)
+        self.steps.leave(self.upper)
+        self.upper_got = lax.ppermute(away, "blk", partner(4))
+        self.lower_got = lax.ppermute(off, "blk", partner(2))
+
+    def four(self, widths):
+        values = self.steps.enter(self.upper, self.upper_got, self.lower, self.lower_got)
+        res = fold_four(widths, *values)
+        self.steps.leave(res[0])
+        return res
 
 
 def inverse(values):
@@ -547,133 +883,146 @@
 ):
     loc, seqs, width = hidden_in.shape
     blocks = block_order.shape[0]
+    rows = seqs * loc
+    units = w_gate.shape[1]
     kv = w_key.shape[1] // HEAD_DIM
     group = w_query.shape[1] // w_key.shape[1]
+    wide = group * HEAD_DIM
     me = lax.axis_index("blk")
     line = lax.axis_index("tp")
     middle = (line == 1) | (line == 2)
     index = jnp.arange(blocks, dtype=jnp.int32)
     at = jnp.sum(jnp.where(block_order[None, :] == index[:, None], index[None, :], 0), axis=1)
     mine = block_order[me] * loc + jnp.arange(loc, dtype=jnp.int32)
+    steps = Steps()
+    enter, leave = steps.enter, steps.leave
 
     x = hidden_in.transpose(1, 0, 2)
     cosine, sine = tables(mine)
     messages, normed = project(x, attn_gain[None, :], cosine, sine, w_query, w_key, w_value)
+    leave(messages)
     rec = lax.all_to_all(messages, "blk", 0, 0, tiled=True)
-    mixed, full, lse = attend(at, rec, group)
+    scales = jnp.where(seq_labels == 1, exit_scales[1], exit_scales[0])
+    cot = enter(d_out).transpose(1, 0, 2).astype(F32) * scales[:, None, None]
+    g_down = leave(cot.astype(BF16).reshape(rows, width))
+    d_hidden = leave(dot_rt(g_down, w_down).astype(BF16))
+    mixed, full, lse = attend(at, enter(rec), group)
+    leave(mixed)
     mixed = lax.all_to_all(mixed, "blk", 0, 0, tiled=True)
-    mixed, parts = out_project(mixed, w_out, seqs)
-    attn = [sum_line(p, middle) for p in parts]
-
-    scales = jnp.where(seq_labels == 1, exit_scales[1], exit_scales[0])
-    cot = d_out.transpose(1, 0, 2).astype(F32) * scales[:, None, None]
-    g_down = cot.astype(BF16)
+    all_cosine, all_sine = tables(enter(jnp.arange(blocks * loc, dtype=jnp.int32)))
+    leave(all_cosine)
+    mixed, parts = out_project(enter(mixed), w_out, seqs)
+    leave(mixed)
+
     gain_m = mlp_gain.astype(F32)
-    norms, hiddens, gates, ups, grads, gains = [], [], [], [], [], []
-    span = 2
-    for first in range(0, seqs, span):
-        part = slice(first, first + span)
-        rows = span * loc
-        total = jnp.concatenate(attn[part], axis=0).astype(F32)
-        resid = x[part].reshape(rows, width).astype(F32) + total
+    attn = Line(steps, middle, parts)
+    back = Line(steps, middle, [None] * seqs)
+    norms, hiddens, gates, ups, gains = ([None] * seqs for _ in range(5))
+
+    def feed(s):
+        total = attn.done[s]
+        resid = x[s].astype(F32) + total.astype(F32)
         unit = resid * inverse(resid)
         norm = (unit * gain_m).astype(BF16)
         gate = dot(norm, w_gate)
         up = dot(norm, w_up)
         sig = jax.nn.sigmoid(gate)
         silu = gate * sig
-        d_hidden = dot_rt(g_down[part].reshape(rows, width), w_down)
-        g_up = (d_hidden * silu).astype(BF16)
-        g_gate = (d_hidden * up * (sig * (1.0 + gate * (1.0 - sig)))).astype(BF16)
+        grad_h = d_hidden[s * loc:(s + 1) * loc].astype(F32)
+        g_up = (grad_h * silu).astype(BF16)
+        g_gate = (grad_h * up * (sig * (1.0 + gate * (1.0 - sig)))).astype(BF16)
         grad = dot_rt(g_gate, w_gate) + dot_rt(g_up, w_up)
-        gains.append(jnp.sum(grad * unit, axis=0))
-        grad = grad.astype(BF16)
-        grads += [grad[i * loc:(i + 1) * loc] for i in range(span)]
-        norms.append(norm)
-        hiddens.append((silu * up).astype(BF16))
-        gates.append(g_gate)
-        ups.append(g_up)
-    norm = jnp.concatenate(norms, axis=0)
-    hidden = jnp.concatenate(hiddens, axis=0)
-    d_mlp = gains[0] + gains[1]
-    d_norm = [sum_line(g, middle) for g in grads]
-
-    d_w_down = dot_lt(hidden, g_down.reshape(seqs * loc, width)).astype(BF16)
-    d_w_down = lax.psum_scatter(d_w_down, "blk", scatter_dimension=1, tiled=True).astype(F32)
-    g_both = jnp.concatenate([jnp.concatenate(gates, axis=0), jnp.concatenate(ups, axis=0)], axis=1)
-    d_w_both = dot_lt(norm, g_both).astype(BF16)
-    d_w_both = lax.psum_scatter(d_w_both, "blk", scatter_dimension=0, tiled=True).astype(F32)
-    units = w_gate.shape[1]
-    d_w_gate, d_w_up = d_w_both[:, :units], d_w_both[:, units:]
-
-    d_resids, g_attns, sends = [], [], []
-    for s in range(seqs):
-        resid = x[s].astype(F32) + attn[s].astype(F32)
+        gains[s] = jnp.sum(grad * unit, axis=0)
+        back.parts[s] = leave(grad.astype(BF16))
+        norms[s], gates[s], ups[s] = norm, g_gate, g_up
+        hiddens[s] = (silu * up).astype(BF16)
+
+    d_resids, g_attns, sends = ([None] * seqs for _ in range(3))
+
+    def norm_back(s):
+        resid = x[s].astype(F32) + attn.done[s].astype(F32)
         inv = inverse(resid)
         unit = resid * inv
-        scaled = d_norm[s].astype(F32) * gain_m
-        d_resid = cot[s] + inv * (scaled - unit * jnp.mean(scaled * unit, axis=-1, keepdims=True))
-        g_attn = d_resid.astype(BF16)
-        g_mixed = dot_rt(g_attn, w_out).astype(BF16)
-        sends += [g_mixed[:, n * group * HEAD_DIM:(n + 1) * group * HEAD_DIM] for n in range(kv)]
-        d_resids.append(d_resid)
-        g_attns.append(g_attn)
-    g_attn = jnp.stack(g_attns)
-    grad = lax.all_to_all(jnp.stack(sends), "blk", 0, 0, tiled=True)
-    cosine, sine = tables(jnp.arange(blocks * loc, dtype=jnp.int32))
-    back = attend_back(at, rec, grad, full, lse, cosine, sine, group)
-    back = lax.all_to_all(back, "blk", 0, 0, tiled=True)
-    back = back.reshape(seqs, kv, loc, (group + 2) * HEAD_DIM)
-
-    out_parts = [dot(hidden[s * loc:(s + 1) * loc], w_down).astype(BF16) for s in range(seqs)]
-    outs = [sum_line(p, middle) for p in out_parts]
-    block_out = jnp.stack(
-        [x[s].astype(F32) + attn[s].astype(F32) + outs[s].astype(F32) for s in range(seqs)], axis=1
-    ).astype(BF16)
-
-    wide = group * HEAD_DIM
-    stacked = jnp.concatenate(
-        [w_query.reshape(width, kv, wide), w_key.reshape(width, kv, HEAD_DIM), w_value.reshape(width, kv, HEAD_DIM)],
-        axis=2,
-    )
-    gain_a = attn_gain.astype(F32)
-    grads, d_attn = [], 0.0
-    for s in range(seqs):
-        grad = sum(dot_rt(back[s, n], stacked[:, n]) for n in range(kv))
-        xs = x[s].astype(F32)
-        d_attn = d_attn + jnp.sum(grad * (xs * inverse(xs)), axis=0)
-        grads.append(grad.astype(BF16))
-    totals = [sum_line(g, middle) for g in grads]
-    d_gains = sum_gain(jnp.stack([d_attn, d_mlp], axis=1))
-
-    d_w_attn = jnp.einsum("srd,snrc->dnc", normed, back, preferred_element_type=F32).astype(BF16)
-    d_w_out = jnp.einsum("srd,src->dc", g_attn, mixed, preferred_element_type=F32).astype(BF16)
-    packed = jnp.concatenate([d_w_attn.reshape(width, -1), d_w_out], axis=1)
-    packed = scatter_sum(packed)
-    cut = kv * (group + 2) * HEAD_DIM
-    d_w_out = packed[:, cut:].T
-    d_w_attn = packed[:, :cut].reshape(-1, kv, (group + 2) * HEAD_DIM)
-    d_w_query = d_w_attn[:, :, :wide].reshape(-1, kv * wide)
-    d_w_key = d_w_attn[:, :, wide:wide + HEAD_DIM].reshape(-1, kv * HEAD_DIM)
-    d_w_value = d_w_attn[:, :, wide + HEAD_DIM:].reshape(-1, kv * HEAD_DIM)
-
-    d_ins = []
-    for s in range(seqs):
-        xs = x[s].astype(F32)
-        inv = inverse(xs)
-        unit = xs * inv
-        scaled = totals[s].astype(F32) * gain_a
-        d_ins.append(d_resids[s] + inv * (scaled - unit * jnp.mean(scaled * unit, axis=-1, keepdims=True)))
-    d_hidden_in = jnp.stack(d_ins, axis=1)
+        scaled = back.done[s].astype(F32) * gain_m
+        d_resids[s] = cot[s] + inv * (scaled - unit * jnp.mean(scaled * unit, axis=-1, keepdims=True))
+        g_attns[s] = d_resids[s].astype(BF16)
+        sends[s] = leave(dot_rt(g_attns[s], w_out).astype(BF16))
+
+    def run(lines, text):
+        for word in text.split():
+            name, c = word[:-1], int(word[-1])
+            if name == "F":
+                feed(c)
+            elif name == "N":
+                norm_back(c)
+            else:
+                obj = lines[name[0]]
+                (obj.one, obj.two, obj.three, obj.four, obj.five)[int(name[1]) - 1](c)
+
+    lines = {"a": attn, "b": back}
+    core = (me % 2).astype(jnp.int32)[None]
+    place = jnp.stack([(me // 2) % 2, me // 4]).astype(jnp.int32)
+    run(lines, "a10 a11 a12 a13 a20 a21 a30 a22 a31 a40 F0 b10 a23 a32 a41 F1 b11")
+    run(lines, "a33 a42 F2 b12 b20 a43 F3 b13 b21 b30")
+    hidden = [enter(jnp.concatenate(hiddens[i:i + 2], axis=0)) for i in range(0, seqs, 2)]
+    outs = Line(steps, middle, [leave(dot(h, w_down).astype(BF16)) for h in hidden])
+    lines["c"] = outs
+    run(lines, "c10 c11 b22 b31 b40 N0 b23 b32 b41 N1 b33 c20 b42 N2 b43 N3")
+    send = jnp.stack(sends).reshape(seqs, loc, kv, wide).transpose(0, 2, 1, 3).reshape(seqs * kv, loc, wide)
+    grad = lax.all_to_all(send, "blk", 0, 0, tiled=True)
+    send, keep = ffn_grads(*enter(core, gates, ups, hiddens, g_down, norms), blocks)
+    leave(keep)
+    ffn_sum = Scatter(steps, place, send, keep)
+    grads = leave(attend_back(at, rec, enter(grad), full, lse, all_cosine, all_sine, group))
+    grads = lax.all_to_all(grads, "blk", 0, 0, tiled=True)
+    run(lines, "c21 c30")
+
+    grads = enter(grads)
+    ins = Line(steps, middle, input_grads(grads, x, w_query, w_key, w_value, [g[None, :] for g in gains]))
+    leave(ins.parts[0])
+    lines["d"] = ins
+    run(lines, "d10 d11 d12 d13")
+    ffn_sum.two()
+    run(lines, "c31 d20 d21 d30 c50")
+    send, keep = attn_grads(*enter(core, grads, mixed, normed, g_attns), kv, blocks)
+    leave(keep)
+    attn_sum = Scatter(steps, place, send, keep)
+    run(lines, "d22 d31 c51")
+    mid = middle.astype(jnp.int32)[None]
+    block_out = leave(block_output(mid, x, attn.done, enter(outs.total), outs.third))
+    attn_sum.two()
+    run(lines, "d40")
+    extra = ins.done[0][loc:loc + 4].astype(F32)
+    both = (extra[0::2] + extra[1::2]).reshape(2, 8, width // 8)
+    both = leave(both + lax.ppermute(both, "blk", partner(1)))
+    others = [lax.ppermute(both, "blk", partner(bit)) for bit in (2, 4, 6)]
+    run(lines, "d23 d32 d51")
+    ffn_sum.three()
+    run(lines, "d33 d52")
+    attn_sum.three()
+    d_w_gate, d_w_up, d_w_down = ffn_sum.four((units, units, units))
+    d_w_query, d_w_key, d_w_value, d_w_out = attn_sum.four((kv * wide, kv * HEAD_DIM, kv * HEAD_DIM, kv * wide))
+    others = enter(others)
+    both = both + others[0] + others[1] + others[2]
+    both = leave(lax.dynamic_index_in_dim(both, me, 1, keepdims=False))
+    ends = enter(ins.third[-1])
+    d_hidden_in = finish(
+        mid,
+        x,
+        attn_gain[None, :],
+        ins.total,
+        ins.third[:-1] + [ends],
+        d_resids,
+    )
     return (
         block_out,
         d_hidden_in,
-        d_gains[:, 0],
+        both[0],
         d_w_query,
         d_w_key,
         d_w_value,
         d_w_out,
-        d_gains[:, 1],
+        both[1],
         d_w_gate,
         d_w_up,
         d_w_down,

time: 692 us -> 456 us (0.66)
  the two profiles are of different devices: /device:TPU:0 before, /device:TPU:14 now
where the time goes in v2:
time: 456 us; the launch traced here: 447 us
  starting transfers between devices  130 us (29%)
  waiting for transfers between devices  126 us (28%)
  Pallas kernels  96.7 us (21%)
  matrix products  40.1 us (9%)
  other arithmetic  26 us (6%)
  local copies, waits for them, and re-layouts  23.7 us (5%)
    ppermute x14, starting transfers between devices, three(): self.third[c] = lax.ppermute(self.total[c], 'tp', [(1, 0), (2, 3)])  44.6 us
    ppermute x14, starting transfers between devices, two(): self.second[c] = lax.ppermute(self.half[c], 'tp', [(1, 2), (2, 1)])  39 us
    ppermute x14, waiting for transfers between devices, one(): self.first[c] = lax.ppermute(self.parts[c], 'tp', [(0, 1), (3, 2)])  38.3 us
    pallas_call x2, Pallas kernels, shares_call(): pl.pallas_call(body, grid_spec=pltpu.PrefetchScalarGridSpec(num_scalar_pr...  26.7 us
    ppermute x14, waiting for transfers between devices, three(): self.third[c] = lax.ppermute(self.total[c], 'tp', [(1, 0), (2, 3)])  26.6 us
    dot_general x13, matrix products, dot_rt(): lax.dot_general(left, right, (((1,), (1,)), ((), ())), preferred_element_...  26.2 us
    ppermute x14, waiting for transfers between devices, two(): self.second[c] = lax.ppermute(self.half[c], 'tp', [(1, 2), (2, 1)])  21.4 us
    unnamed x182, local copies, waits for them, and re-layouts  21 us
  transfers between devices with their start and end apart: 60, of which 28 were waited for; matrix products, arithmetic and copies ran while one was open for 14% of the time, Pallas kernels for 14%

profile of v2, /device:TPU:14, one launch (start us, length us, event | category | flops | bytes accessed | tf_op | source)
XLA Modules:
  0.0 446.7 jit_solution(4953513646498281856)
XLA Ops:
  11.4 4.2 all-to-all-start
  17.5 5.0 %multiply_bitcast_fusion = (f32[4,128,2048]{2,1,0:T(8,128)}, bf16[4,128,2048]{2,1,0:T(8,128)(2,1)S(1)}) fusion(bf16[128,4,2048]{2,1,0:T(4,128)(2,1)} %param.27, f32[4]{0:T(128)S(1)} %compare_select_fusion), kind=kLoop, calls=%fused_computation | loop fusion | flops 3145728 | bytes 8388624 | tf_op jit(solution)/shard_map/mul | solution.py:906
  23.8 7.2 %convolution_convert_fusion = bf16[512,1408]{1,0:T(8,128)(2,1)} fusion(bf16[512,2048]{1,0:T(8,128)(2,1)S(1)} %bitcast.227, bf16[1408,2048]{1,0:T(8,128)(2,1)} %param.26), kind=kOutput, calls=%fused_computation.1 | convolution fusion | flops 2953510912 | bytes 9306112 | tf_op jit(solution)/shard_map/dot_general | solution.py:25
  37.6 4.5 %all-to-all-start.1 = ((bf16[8,128,256]{2,1,0:T(8,128)(2,1)}), bf16[8,128,256]{2,1,0:T(8,128)(2,1)S(1)}, u32[]{:S(2)}, u32[]{:S(2)}) async-start(bf16[8,128,256]{2,1,0:T(8,128)(2,1)} %copy-done.25), calls=%async_computation.1 | async-start | bytes 1048576 | tf_op jit(solution)/shard_map/all_to_all | solution.py:911
  55.3 14.1 %collective-permute-done.right = bf16[128,2048]{1,0:T(8,128)(2,1)S(1)} collective-permute-done((bf16[128,2048]{1,0:T(8,128)(2,1)S(1)}, bf16[128,2048]{1,0:T(8,128)(2,1)S(1)}, u32[]{:S(2)}, u32[]{:S(2)}) %collective-permute-start) | collective-permute-done | bytes 524320 | tf_op jit(solution)/shard_map/ppermute | solution.py:809
  122.4 4.6 %collective-permute-start.11 = (bf16[128,2048]{1,0:T(8,128)(2,1)S(1)}, bf16[128,2048]{1,0:T(8,128)(2,1)S(1)}, u32[]{:S(2)}, u32[]{:S(2)}) collective-permute-start(bf16[128,2048]{1,0:T(8,128)(2,1)S(1)} %shard_map.231), channel_id=1, source_target_pairs={{1,0},{2,3},{5,4},{6,7},{9,8},{10,11},{13,12},{14,15},{17,16},{18,... | collective-permute-start | bytes 1572872 | tf_op jit(solution)/shard_map/ppermute | solution.py:819
  161.8 4.9 %collective-permute-start.21 = (bf16[128,2048]{1,0:T(8,128)(2,1)S(1)}, bf16[128,2048]{1,0:T(8,128)(2,1)S(1)}, u32[]{:S(2)}, u32[]{:S(2)}) collective-permute-start(bf16[128,2048]{1,0:T(8,128)(2,1)S(1)} %shard_map.236), channel_id=1, source_target_pairs={{1,0},{2,3},{5,4},{6,7},{9,8},{10,11},{13,12},{14,15},{17,16},{18,... | collective-permute-start | bytes 1572872 | tf_op jit(solution)/shard_map/ppermute | solution.py:819
  174.4 4.6 %collective-permute-done.21 = bf16[128,2048]{1,0:T(8,128)(2,1)S(1)} collective-permute-done((bf16[128,2048]{1,0:T(8,128)(2,1)S(1)}, bf16[128,2048]{1,0:T(8,128)(2,1)S(1)}, u32[]{:S(2)}, u32[]{:S(2)}) %collective-permute-start.21) | collective-permute-done | bytes 524320 | tf_op jit(solution)/shard_map/ppermute | solution.py:819
  182.7 4.4 collective-permute-start.26
  199.4 17.8 %shard_map.241 = (bf16[4,256,4224]{2,1,0:T(8,128)(2,1)}, bf16[4,256,4224]{2,1,0:T(8,128)(2,1)}) custom-call(s32[1]{0:T(128)} %bitcast.20.core_ref, bf16[128,1408]{1,0:T(8,128)(2,1)S(1)} %get-tuple-element.253.refs_0_, bf16[128,1408]{1,0:T(8,128)(2,1)S(1)} %get-tuple-element.254.refs_1_, bf16[128,1408]{1,0:T(8,128)(2,1)S(1)} %get-tuple-element.255.refs_2_, ...), custom_call_target="tpu_custom_call" | custom-call | flops 5000000000 | bytes 1000000 | tf_op jit(solution)/shard_map/pallas_call | solution.py:295
  219.7 4.6 %all-to-all-start.2 = ((bf16[8,128,256]{2,1,0:T(8,128)(2,1)}), bf16[8,128,256]{2,1,0:T(8,128)(2,1)}, u32[]{:S(2)}, u32[]{:S(2)}) async-start(bf16[8,128,256]{2,1,0:T(8,128)(2,1)} %bitcast.226), calls=%async_computation.2 | async-start | bytes 1048576 | tf_op jit(solution)/shard_map/all_to_all | solution.py:972
  231.8 7.6 %shard_map.242 = bf16[8,128,512]{2,1,0:T(8,128)(2,1)} custom-call(s32[8]{0:T(128)} %copy-done.66, bf16[8,128,512]{2,1,0:T(8,128)(2,1)} %copy-done.17, bf16[8,128,256]{2,1,0:T(8,128)(2,1)} %all-to-all-done.2.grad_ref, f32[8,256,128]{2,1,0:T(8,128)} %copy-done.69, f32[8,256,128]{2,1,0:T(8,128)} %copy-done.70, f32[1024,128]{1,0:T(8,128)} %pad_maximum_fusion.2.cos_ref, ...), custom_call_target="tpu_custom_call" | custom-call | flops 5000000000 | bytes 1000000 | tf_op jit(solution)/shard_map/pallas_call | solution.py:182
  239.4 5.9 %all-to-all-start.3 = ((bf16[8,128,512]{2,1,0:T(8,128)(2,1)}), bf16[8,128,512]{2,1,0:T(8,128)(2,1)S(1)}, u32[]{:S(2)}, u32[]{:S(2)}) async-start(bf16[8,128,512]{2,1,0:T(8,128)(2,1)} %shard_map.242), calls=%async_computation.3 | async-start | bytes 2097152 | tf_op jit(solution)/shard_map/all_to_all | solution.py:977
  254.0 4.4 all-to-all-done.3.back_ref
  259.3 7.2 %shard_map.245 = (bf16[144,2048]{1,0:T(8,128)(2,1)}, bf16[128,2048]{1,0:T(8,128)(2,1)}, bf16[128,2048]{1,0:T(8,128)(2,1)}, bf16[128,2048]{1,0:T(8,128)(2,1)}) custom-call(bf16[8,128,512]{2,1,0:T(8,128)(2,1)} %copy-done.18, bf16[4,128,2048]{2,1,0:T(8,128)(2,1)} %bitcast.191, bf16[2048,512]{1,0:T(8,128)(2,1)} %wq_ref.3, bf16[2048,256]{1,0:T(8,128)(2,1)} %wk_ref.3, ...), custom_call_target="tpu_custom_call" | custom-call | flops 5000000000 | bytes 1000000 | tf_op jit(solution)/shard_map/pallas_call | solution.py:268
  269.1 8.8 %shard_map.246 = (bf16[2,128,4224]{2,1,0:T(8,128)(2,1)S(1)}, bf16[2,128,4224]{2,1,0:T(8,128)(2,1)S(1)}, bf16[2,128,4224]{2,1,0:T(8,128)(2,1)}, bf16[2,128,4224]{2,1,0:T(8,128)(2,1)S(1)}) custom-call(s32[2]{0:T(128)S(1)} %pad_add_fusion.place_ref, bf16[2,2,256,4224]{3,2,1,0:T(8,128)(2,1)} %bitcast.220, bf16[2,2,256,4224]{3,2,1,0:T(8,128)(2,1)} %bitcast.221, ...), custom_call_target="tpu_custom_call" | custom-call | flops 5000000000 | bytes 1000000 | tf_op jit(solution)/shard_map/pallas_call | solution.py:393
  277.9 4.4 shard_map.247.refs_6_.refs_7_
  289.3 6.8 %collective-permute-done.30.right = bf16[128,2048]{1,0:T(8,128)(2,1)S(1)} collective-permute-done((bf16[128,2048]{1,0:T(8,128)(2,1)}, bf16[128,2048]{1,0:T(8,128)(2,1)S(1)}, u32[]{:S(2)}, u32[]{:S(2)}) %collective-permute-start.30) | collective-permute-done | bytes 524320 | tf_op jit(solution)/shard_map/ppermute | solution.py:809
  296.3 5.0 %collective-permute-done.35.right = bf16[144,2048]{1,0:T(8,128)(2,1)S(1)} collective-permute-done((bf16[144,2048]{1,0:T(8,128)(2,1)S(1)}, bf16[144,2048]{1,0:T(8,128)(2,1)S(1)}, u32[]{:S(2)}, u32[]{:S(2)}) %collective-permute-start.35) | collective-permute-done | bytes 589856 | tf_op jit(solution)/shard_map/ppermute | solution.py:814
  301.5 10.0 %collective-permute-done.34.refs_8_.refs_9_ = bf16[256,2048]{1,0:T(8,128)(2,1)S(1)} collective-permute-done((bf16[256,2048]{1,0:T(8,128)(2,1)S(1)}, bf16[256,2048]{1,0:T(8,128)(2,1)S(1)}, u32[]{:S(2)}, u32[]{:S(2)}) %collective-permute-start.34) | collective-permute-done | bytes 1048608 | tf_op jit(solution)/shard_map/ppermute | solution.py:819
  312.5 8.8 %shard_map.251 = (bf16[4,256,1536]{2,1,0:T(8,128)(2,1)}, bf16[4,256,1536]{2,1,0:T(8,128)(2,1)}) custom-call(s32[1]{0:T(128)} %bitcast.20.core_ref, bf16[8,128,512]{2,1,0:T(8,128)(2,1)S(1)} %copy-done.19, bf16[4,128,512]{2,1,0:T(8,128)(2,1)S(1)} %copy-done.72, bf16[4,128,2048]{2,1,0:T(8,128)(2,1)S(1)} %copy-done.68, bf16[128,2048]{1,0:T(8,128)(2,1)S(1)} %copy-done.10, ...), custom_call_target="tpu_custom_call" | custom-call | flops 5000000000 | bytes 1000000 | tf_op jit(solution)/shard_map/pallas_call | solution.py:295
  322.6 5.6 %collective-permute-start.29 = (bf16[256,2048]{1,0:T(8,128)(2,1)}, bf16[256,2048]{1,0:T(8,128)(2,1)}, u32[]{:S(2)}, u32[]{:S(2)}) collective-permute-start(bf16[256,2048]{1,0:T(8,128)(2,1)} %shard_map.247.refs_6_.refs_7_), channel_id=1, source_target_pairs={{1,0},{2,3},{5,4},{6,7},{9,8},{10,11},{13,12},{14,15},{17,16},{18,... | collective-permute-start | bytes 3145736 | tf_op jit(solution)/shard_map/ppermute | solution.py:819
  332.0 5.9 %collective-permute-done.33.right = bf16[128,2048]{1,0:T(8,128)(2,1)S(1)} collective-permute-done((bf16[128,2048]{1,0:T(8,128)(2,1)S(1)}, bf16[128,2048]{1,0:T(8,128)(2,1)S(1)}, u32[]{:S(2)}, u32[]{:S(2)}) %collective-permute-start.33) | collective-permute-done | bytes 524320 | tf_op jit(solution)/shard_map/ppermute | solution.py:809
  338.8 5.1 %collective-permute-done.32.right = bf16[128,2048]{1,0:T(8,128)(2,1)S(1)} collective-permute-done((bf16[128,2048]{1,0:T(8,128)(2,1)S(1)}, bf16[128,2048]{1,0:T(8,128)(2,1)S(1)}, u32[]{:S(2)}, u32[]{:S(2)}) %collective-permute-start.32) | collective-permute-done | bytes 524320 | tf_op jit(solution)/shard_map/ppermute | solution.py:814
  350.4 4.6 %collective-permute-start.38 = (bf16[144,2048]{1,0:T(8,128)(2,1)S(1)}, bf16[144,2048]{1,0:T(8,128)(2,1)S(1)}, u32[]{:S(2)}, u32[]{:S(2)}) collective-permute-start(bf16[144,2048]{1,0:T(8,128)(2,1)S(1)} %copy-done.29), channel_id=1, source_target_pairs={{1,0},{2,3},{5,4},{6,7},{9,8},{10,11},{13,12},{14,15},{17,16},{18,... | collective-permute-start | bytes 1769480 | tf_op jit(solution)/shard_map/ppermute | solution.py:819
  355.0 5.5 %shard_map.254 = bf16[128,4,2048]{2,1,0:T(4,128)(2,1)} custom-call(s32[1]{0:T(128)} %bitcast.mid_ref, bf16[4,128,2048]{2,1,0:T(8,128)(2,1)S(1)} %bitcast.192, bf16[128,2048]{1,0:T(8,128)(2,1)S(1)} %get-tuple-element.390.refs_0_, bf16[128,2048]{1,0:T(8,128)(2,1)S(1)} %get-tuple-element.388.refs_1_, bf16[128,2048]{1,0:T(8,128)(2,1)S(1)} %copy-done.6, ...), custom_call_target="tpu_custom_call" | custom-call | flops 5000000000 | bytes 1000000 | tf_op jit(solution)/shard_map/pallas_call | solution.py:500
  375.1 9.3 %collective-permute-done.36.right = bf16[128,2048]{1,0:T(8,128)(2,1)S(1)} collective-permute-done((bf16[128,2048]{1,0:T(8,128)(2,1)}, bf16[128,2048]{1,0:T(8,128)(2,1)S(1)}, u32[]{:S(2)}, u32[]{:S(2)}) %collective-permute-start.36) | collective-permute-done | bytes 524320 | tf_op jit(solution)/shard_map/ppermute | solution.py:814
  401.9 4.4 collective-permute-start.46
  406.4 5.5 %collective-permute-done.51 = bf16[2,128,1536]{2,1,0:T(8,128)(2,1)S(1)} collective-permute-done((bf16[2,128,1536]{2,1,0:T(8,128)(2,1)S(1)}, bf16[2,128,1536]{2,1,0:T(8,128)(2,1)S(1)}, u32[]{:S(2)}, u32[]{:S(2)}) %collective-permute-start.51) | collective-permute-done | bytes 786464 | tf_op jit(solution)/shard_map/ppermute | solution.py:843
  416.3 4.6 %shard_map.260 = f32[128,4,2048]{2,1,0:T(4,128)} custom-call(s32[1]{0:T(128)} %bitcast.mid_ref, bf16[4,128,2048]{2,1,0:T(8,128)(2,1)S(1)} %bitcast.193, bf16[1,2048]{1,0:T(2,128)(2,1)S(1)} %copy-done.27, bf16[144,2048]{1,0:T(8,128)(2,1)S(1)} %copy-done.30, bf16[128,2048]{1,0:T(8,128)(2,1)S(1)} %copy-done.55, bf16[128,2048]{1,0:T(8,128)(2,1)S(1)} %shard_map.257.refs_2_, ...), custom_call_target="tpu_custom_call" | custom-call | flops 5000000000 | bytes 1000000 | tf_op jit(solution)/shard_map/pallas_call | solution.py:471
  420.9 12.9 %collective-permute-done.54.upper_got = bf16[128,4224]{1,0:T(8,128)(2,1)S(1)} collective-permute-done((bf16[128,4224]{1,0:T(8,128)(2,1)S(1)}, bf16[128,4224]{1,0:T(8,128)(2,1)S(1)}, u32[]{:S(2)}, u32[]{:S(2)}) %collective-permute-start.54) | collective-permute-done | bytes 1081376 | tf_op jit(solution)/shard_map/ppermute | solution.py:849
  438.3 4.9 %collective-permute-done.52.upper_got = bf16[128,1536]{1,0:T(8,128)(2,1)S(1)} collective-permute-done((bf16[128,1536]{1,0:T(8,128)(2,1)S(1)}, bf16[128,1536]{1,0:T(8,128)(2,1)S(1)}, u32[]{:S(2)}, u32[]{:S(2)}) %collective-permute-start.52) | collective-permute-done | bytes 393248 | tf_op jit(solution)/shard_map/ppermute | solution.py:849
  (392 shorter events, 230.3 us)
Async XLA Ops:
  11.4 19.6 %all-to-all-start = ((bf16[8,128,512]{2,1,0:T(8,128)(2,1)}), bf16[8,128,512]{2,1,0:T(8,128)(2,1)S(1)}, u32[]{:S(2)}, u32[]{:S(2)}) async-start(bf16[8,128,512]{2,1,0:T(8,128)(2,1)} %copy-done.20), calls=%async_computation | async-start | bytes 2097152 | tf_op jit(solution)/shard_map/all_to_all | solution.py:904
  54.0 26.6 %collective-permute-start.2 = (bf16[128,2048]{1,0:T(8,128)(2,1)}, bf16[128,2048]{1,0:T(8,128)(2,1)S(1)}, u32[]{:S(2)}, u32[]{:S(2)}) collective-permute-start(bf16[128,2048]{1,0:T(8,128)(2,1)} %get-tuple-element.200.left), channel_id=1, source_target_pairs={{0,1},{3,2},{4,5},{7,6},{8,9},{11,10},{12,13},{15,14},{16,17},{19,... | collective-permute-start | bytes 1572872 | tf_op jit(solution)/shard_map/ppermute | solution.py:809
  73.8 18.0 %collective-permute-start.5 = (bf16[128,2048]{1,0:T(8,128)(2,1)}, bf16[128,2048]{1,0:T(8,128)(2,1)S(1)}, u32[]{:S(2)}, u32[]{:S(2)}) collective-permute-start(bf16[128,2048]{1,0:T(8,128)(2,1)} %copy-done.59), channel_id=1, source_target_pairs={{0,1},{3,2},{4,5},{7,6},{8,9},{11,10},{12,13},{15,14},{16,17},{19,... | collective-permute-start | bytes 1572872 | tf_op jit(solution)/shard_map/ppermute | solution.py:809
  75.1 32.7 %collective-permute-start.8 = (bf16[128,2048]{1,0:T(8,128)(2,1)S(1)}, bf16[128,2048]{1,0:T(8,128)(2,1)S(1)}, u32[]{:S(2)}, u32[]{:S(2)}) collective-permute-start(bf16[128,2048]{1,0:T(8,128)(2,1)S(1)} %get-tuple-element.212.left), channel_id=1, source_target_pairs={{0,1},{3,2},{4,5},{7,6},{8,9},{11,10},{12,13},{15,14},{16,17},{19,... | collective-permute-start | bytes 1572872 | tf_op jit(solution)/shard_map/ppermute | solution.py:809
  92.0 18.0 %collective-permute-start.7 = (bf16[128,2048]{1,0:T(8,128)(2,1)S(1)}, bf16[128,2048]{1,0:T(8,128)(2,1)S(1)}, u32[]{:S(2)}, u32[]{:S(2)}) collective-permute-start(bf16[128,2048]{1,0:T(8,128)(2,1)S(1)} %shard_map.227.left), channel_id=1, source_target_pairs={{1,2},{2,1},{5,6},{6,5},{9,10},{10,9},{13,14},{14,13},{17,18},{18,... | collective-permute-start | bytes 1572872 | tf_op jit(solution)/shard_map/ppermute | solution.py:814
  96.4 17.5 %collective-permute-start.6 = (bf16[128,2048]{1,0:T(8,128)(2,1)S(1)}, bf16[128,2048]{1,0:T(8,128)(2,1)S(1)}, u32[]{:S(2)}, u32[]{:S(2)}) collective-permute-start(bf16[128,2048]{1,0:T(8,128)(2,1)S(1)} %shard_map.228), channel_id=1, source_target_pairs={{1,0},{2,3},{5,4},{6,7},{9,8},{10,11},{13,12},{14,15},{17,16},{18,... | collective-permute-start | bytes 1572872 | tf_op jit(solution)/shard_map/ppermute | solution.py:819
  106.5 28.7 %collective-permute-start.12 = (bf16[128,2048]{1,0:T(8,128)(2,1)S(1)}, bf16[128,2048]{1,0:T(8,128)(2,1)S(1)}, u32[]{:S(2)}, u32[]{:S(2)}) collective-permute-start(bf16[128,2048]{1,0:T(8,128)(2,1)S(1)} %get-tuple-element.222.left), channel_id=1, source_target_pairs={{0,1},{3,2},{4,5},{7,6},{8,9},{11,10},{12,13},{15,14},{16,17},{19,... | collective-permute-start | bytes 1572872 | tf_op jit(solution)/shard_map/ppermute | solution.py:809
  120.9 24.9 %collective-permute-start.14 = (bf16[128,2048]{1,0:T(8,128)(2,1)S(1)}, bf16[128,2048]{1,0:T(8,128)(2,1)S(1)}, u32[]{:S(2)}, u32[]{:S(2)}) collective-permute-start(bf16[128,2048]{1,0:T(8,128)(2,1)S(1)} %get-tuple-element.226.left), channel_id=1, source_target_pairs={{0,1},{3,2},{4,5},{7,6},{8,9},{11,10},{12,13},{15,14},{16,17},{19,... | collective-permute-start | bytes 1572872 | tf_op jit(solution)/shard_map/ppermute | solution.py:809
  133.9 20.7 %collective-permute-start.19 = (bf16[128,2048]{1,0:T(8,128)(2,1)S(1)}, bf16[128,2048]{1,0:T(8,128)(2,1)S(1)}, u32[]{:S(2)}, u32[]{:S(2)}) collective-permute-start(bf16[128,2048]{1,0:T(8,128)(2,1)S(1)} %get-tuple-element.232.left), channel_id=1, source_target_pairs={{0,1},{3,2},{4,5},{7,6},{8,9},{11,10},{12,13},{15,14},{16,17},{19,... | collective-permute-start | bytes 1572872 | tf_op jit(solution)/shard_map/ppermute | solution.py:809
  144.5 26.0 %collective-permute-start.16 = (bf16[128,2048]{1,0:T(8,128)(2,1)S(1)}, bf16[128,2048]{1,0:T(8,128)(2,1)S(1)}, u32[]{:S(2)}, u32[]{:S(2)}) collective-permute-start(bf16[128,2048]{1,0:T(8,128)(2,1)S(1)} %get-tuple-element.238.left), channel_id=1, source_target_pairs={{0,1},{3,2},{4,5},{7,6},{8,9},{11,10},{12,13},{15,14},{16,17},{19,... | collective-permute-start | bytes 1572872 | tf_op jit(solution)/shard_map/ppermute | solution.py:809
  154.8 17.9 %collective-permute-start.22 = (bf16[128,2048]{1,0:T(8,128)(2,1)S(1)}, bf16[128,2048]{1,0:T(8,128)(2,1)S(1)}, u32[]{:S(2)}, u32[]{:S(2)}) collective-permute-start(bf16[128,2048]{1,0:T(8,128)(2,1)S(1)} %shard_map.235.left), channel_id=1, source_target_pairs={{1,2},{2,1},{5,6},{6,5},{9,10},{10,9},{13,14},{14,13},{17,18},{18,... | collective-permute-start | bytes 1572872 | tf_op jit(solution)/shard_map/ppermute | solution.py:814
  160.4 26.7 %collective-permute-start.15 = (bf16[256,2048]{1,0:T(8,128)(2,1)S(1)}, bf16[256,2048]{1,0:T(8,128)(2,1)S(1)}, u32[]{:S(2)}, u32[]{:S(2)}) collective-permute-start(bf16[256,2048]{1,0:T(8,128)(2,1)S(1)} %convolution_convert_fusion.2.left), channel_id=1, source_target_pairs={{0,1},{3,2},{4,5},{7,6},{8,9},{11,10},{12,13},{15,14},{16,17},{19,... | collective-permute-start | bytes 3145736 | tf_op jit(solution)/shard_map/ppermute | solution.py:809
  217.2 51.8 %collective-permute-start.28 = (bf16[4,256,4224]{2,1,0:T(8,128)(2,1)}, bf16[4,256,4224]{2,1,0:T(8,128)(2,1)}, u32[]{:S(2)}, u32[]{:S(2)}) collective-permute-start(bf16[4,256,4224]{2,1,0:T(8,128)(2,1)} %get-tuple-element.278), channel_id=1, source_target_pairs={{0,4},{4,0},{8,12},{12,8},{16,20},{20,16},{24,28},{28,24},{1,5},{5... | collective-permute-start | bytes 25952264 | tf_op jit(solution)/shard_map/ppermute | solution.py:836
  217.3 27.9 %collective-permute-start.24 = (bf16[256,2048]{1,0:T(8,128)(2,1)}, bf16[256,2048]{1,0:T(8,128)(2,1)}, u32[]{:S(2)}, u32[]{:S(2)}) collective-permute-start(bf16[256,2048]{1,0:T(8,128)(2,1)} %convolution_convert_fusion.1.left), channel_id=1, source_target_pairs={{0,1},{3,2},{4,5},{7,6},{8,9},{11,10},{12,13},{15,14},{16,17},{19,... | collective-permute-start | bytes 3145736 | tf_op jit(solution)/shard_map/ppermute | solution.py:809
  224.3 27.2 %collective-permute-start.23 = (bf16[256,2048]{1,0:T(8,128)(2,1)S(1)}, bf16[256,2048]{1,0:T(8,128)(2,1)}, u32[]{:S(2)}, u32[]{:S(2)}) collective-permute-start(bf16[256,2048]{1,0:T(8,128)(2,1)S(1)} %copy-done.42), channel_id=1, source_target_pairs={{1,2},{2,1},{5,6},{6,5},{9,10},{10,9},{13,14},{14,13},{17,18},{18,... | collective-permute-start | bytes 3145736 | tf_op jit(solution)/shard_map/ppermute | solution.py:814
  239.4 18.9 %all-to-all-start.3 = ((bf16[8,128,512]{2,1,0:T(8,128)(2,1)}), bf16[8,128,512]{2,1,0:T(8,128)(2,1)S(1)}, u32[]{:S(2)}, u32[]{:S(2)}) async-start(bf16[8,128,512]{2,1,0:T(8,128)(2,1)} %shard_map.242), calls=%async_computation.3 | async-start | bytes 2097152 | tf_op jit(solution)/shard_map/all_to_all | solution.py:977
  248.0 29.9 %collective-permute-start.27 = (bf16[256,2048]{1,0:T(8,128)(2,1)}, bf16[256,2048]{1,0:T(8,128)(2,1)}, u32[]{:S(2)}, u32[]{:S(2)}) collective-permute-start(bf16[256,2048]{1,0:T(8,128)(2,1)} %shard_map.243.left), channel_id=1, source_target_pairs={{1,2},{2,1},{5,6},{6,5},{9,10},{10,9},{13,14},{14,13},{17,18},{18,... | collective-permute-start | bytes 3145736 | tf_op jit(solution)/shard_map/ppermute | solution.py:814
  266.5 19.3 %collective-permute-start.31 = (bf16[144,2048]{1,0:T(8,128)(2,1)}, bf16[144,2048]{1,0:T(8,128)(2,1)S(1)}, u32[]{:S(2)}, u32[]{:S(2)}) collective-permute-start(bf16[144,2048]{1,0:T(8,128)(2,1)} %get-tuple-element.287.left), channel_id=1, source_target_pairs={{0,1},{3,2},{4,5},{7,6},{8,9},{11,10},{12,13},{15,14},{16,17},{19,... | collective-permute-start | bytes 1769480 | tf_op jit(solution)/shard_map/ppermute | solution.py:809
  267.8 28.3 %collective-permute-start.30 = (bf16[128,2048]{1,0:T(8,128)(2,1)}, bf16[128,2048]{1,0:T(8,128)(2,1)S(1)}, u32[]{:S(2)}, u32[]{:S(2)}) collective-permute-start(bf16[128,2048]{1,0:T(8,128)(2,1)} %get-tuple-element.289.left), channel_id=1, source_target_pairs={{0,1},{3,2},{4,5},{7,6},{8,9},{11,10},{12,13},{15,14},{16,17},{19,... | collective-permute-start | bytes 1572872 | tf_op jit(solution)/shard_map/ppermute | solution.py:809
  288.0 23.5 %collective-permute-start.34 = (bf16[256,2048]{1,0:T(8,128)(2,1)S(1)}, bf16[256,2048]{1,0:T(8,128)(2,1)S(1)}, u32[]{:S(2)}, u32[]{:S(2)}) collective-permute-start(bf16[256,2048]{1,0:T(8,128)(2,1)S(1)} %copy-done.44), channel_id=1, source_target_pairs={{1,0},{2,3},{5,4},{6,7},{9,8},{10,11},{13,12},{14,15},{17,16},{18,... | collective-permute-start | bytes 3145736 | tf_op jit(solution)/shard_map/ppermute | solution.py:819
  321.3 39.2 %collective-permute-start.39 = (bf16[4,256,1536]{2,1,0:T(8,128)(2,1)}, bf16[4,256,1536]{2,1,0:T(8,128)(2,1)}, u32[]{:S(2)}, u32[]{:S(2)}) collective-permute-start(bf16[4,256,1536]{2,1,0:T(8,128)(2,1)} %get-tuple-element.313), channel_id=1, source_target_pairs={{0,4},{4,0},{8,12},{12,8},{16,20},{20,16},{24,28},{28,24},{1,5},{5... | collective-permute-start | bytes 9437192 | tf_op jit(solution)/shard_map/ppermute | solution.py:836
  322.6 27.8 %collective-permute-start.29 = (bf16[256,2048]{1,0:T(8,128)(2,1)}, bf16[256,2048]{1,0:T(8,128)(2,1)}, u32[]{:S(2)}, u32[]{:S(2)}) collective-permute-start(bf16[256,2048]{1,0:T(8,128)(2,1)} %shard_map.247.refs_6_.refs_7_), channel_id=1, source_target_pairs={{1,0},{2,3},{5,4},{6,7},{9,8},{10,11},{13,12},{14,15},{17,16},{18,... | collective-permute-start | bytes 3145736 | tf_op jit(solution)/shard_map/ppermute | solution.py:819
  330.7 43.0 %collective-permute-start.37 = (bf16[128,2048]{1,0:T(8,128)(2,1)}, bf16[128,2048]{1,0:T(8,128)(2,1)}, u32[]{:S(2)}, u32[]{:S(2)}) collective-permute-start(bf16[128,2048]{1,0:T(8,128)(2,1)} %get-tuple-element.319.left), channel_id=1, source_target_pairs={{0,1},{3,2},{4,5},{7,6},{8,9},{11,10},{12,13},{15,14},{16,17},{19,... | collective-permute-start | bytes 1572872 | tf_op jit(solution)/shard_map/ppermute | solution.py:809
  337.9 51.4 %collective-permute-start.42 = (bf16[2,128,4224]{2,1,0:T(8,128)(2,1)}, bf16[2,128,4224]{2,1,0:T(8,128)(2,1)}, u32[]{:S(2)}, u32[]{:S(2)}) collective-permute-start(bf16[2,128,4224]{2,1,0:T(8,128)(2,1)} %copy-done.37), channel_id=1, source_target_pairs={{0,8},{4,12},{8,0},{12,4},{16,24},{20,28},{24,16},{28,20},{1,9},{5... | collective-permute-start | bytes 6488072 | tf_op jit(solution)/shard_map/ppermute | solution.py:842
  344.8 50.4 %collective-permute-start.43 = (bf16[2,128,4224]{2,1,0:T(8,128)(2,1)}, bf16[2,128,4224]{2,1,0:T(8,128)(2,1)}, u32[]{:S(2)}, u32[]{:S(2)}) collective-permute-start(bf16[2,128,4224]{2,1,0:T(8,128)(2,1)} %get-tuple-element.325), channel_id=1, source_target_pairs={{0,16},{4,20},{8,24},{12,28},{16,0},{20,4},{24,8},{28,12},{1,17},{... | collective-permute-start | bytes 6488072 | tf_op jit(solution)/shard_map/ppermute | solution.py:843
  373.7 32.6 %collective-permute-start.50 = (bf16[2,128,1536]{2,1,0:T(8,128)(2,1)}, bf16[2,128,1536]{2,1,0:T(8,128)(2,1)S(1)}, u32[]{:S(2)}, u32[]{:S(2)}) collective-permute-start(bf16[2,128,1536]{2,1,0:T(8,128)(2,1)} %copy-done.52), channel_id=1, source_target_pairs={{0,8},{4,12},{8,0},{12,4},{16,24},{20,28},{24,16},{28,20},{1,9},{5... | collective-permute-start | bytes 2359304 | tf_op jit(solution)/shard_map/ppermute | solution.py:842
  387.1 24.8 %collective-permute-start.51 = (bf16[2,128,1536]{2,1,0:T(8,128)(2,1)S(1)}, bf16[2,128,1536]{2,1,0:T(8,128)(2,1)S(1)}, u32[]{:S(2)}, u32[]{:S(2)}) collective-permute-start(bf16[2,128,1536]{2,1,0:T(8,128)(2,1)S(1)} %get-tuple-element.337), channel_id=1, source_target_pairs={{0,16},{4,20},{8,24},{12,28},{16,0},{20,4},{24,8},{28,12},{1,17},{... | collective-permute-start | bytes 2359304 | tf_op jit(solution)/shard_map/ppermute | solution.py:843
  398.4 35.4 %collective-permute-start.54 = (bf16[128,4224]{1,0:T(8,128)(2,1)S(1)}, bf16[128,4224]{1,0:T(8,128)(2,1)S(1)}, u32[]{:S(2)}, u32[]{:S(2)}) collective-permute-start(bf16[128,4224]{1,0:T(8,128)(2,1)S(1)} %bitcast.203), channel_id=1, source_target_pairs={{0,16},{4,20},{8,24},{12,28},{16,0},{20,4},{24,8},{28,12},{1,17},{... | collective-permute-start | bytes 3244040 | tf_op jit(solution)/shard_map/ppermute | solution.py:849
  400.2 35.4 %collective-permute-start.55 = (bf16[128,4224]{1,0:T(8,128)(2,1)S(1)}, bf16[128,4224]{1,0:T(8,128)(2,1)S(1)}, u32[]{:S(2)}, u32[]{:S(2)}) collective-permute-start(bf16[128,4224]{1,0:T(8,128)(2,1)S(1)} %bitcast.202), channel_id=1, source_target_pairs={{0,8},{4,12},{8,0},{12,4},{16,24},{20,28},{24,16},{28,20},{1,9},{5... | collective-permute-start | bytes 3244040 | tf_op jit(solution)/shard_map/ppermute | solution.py:850
  406.3 39.5 %collective-permute-start.47 = (f32[2,8,256]{2,1,0:T(8,128)S(1)}, f32[2,8,256]{2,1,0:T(8,128)S(1)}, u32[]{:S(2)}, u32[]{:S(2)}) collective-permute-start(f32[2,8,256]{2,1,0:T(8,128)S(1)} %fusion.27), channel_id=1, source_target_pairs={{0,8},{4,12},{8,0},{12,4},{16,24},{20,28},{24,16},{28,20},{1,9},{5... | collective-permute-start | bytes 49160 | tf_op jit(solution)/shard_map/ppermute | solution.py:998
  411.9 34.0 %collective-permute-start.48 = (f32[2,8,256]{2,1,0:T(8,128)S(1)}, f32[2,8,256]{2,1,0:T(8,128)S(1)}, u32[]{:S(2)}, u32[]{:S(2)}) collective-permute-start(f32[2,8,256]{2,1,0:T(8,128)S(1)} %fusion.27), channel_id=1, source_target_pairs={{0,16},{4,20},{8,24},{12,28},{16,0},{20,4},{24,8},{28,12},{1,17},{... | collective-permute-start | bytes 49160 | tf_op jit(solution)/shard_map/ppermute | solution.py:998
  415.9 30.0 %collective-permute-start.49 = (f32[2,8,256]{2,1,0:T(8,128)S(1)}, f32[2,8,256]{2,1,0:T(8,128)S(1)}, u32[]{:S(2)}, u32[]{:S(2)}) collective-permute-start(f32[2,8,256]{2,1,0:T(8,128)S(1)} %fusion.27), channel_id=1, source_target_pairs={{0,24},{4,28},{8,16},{12,20},{16,8},{20,12},{24,0},{28,4},{1,25},{... | collective-permute-start | bytes 49160 | tf_op jit(solution)/shard_map/ppermute | solution.py:998
  (118 other events, 1342.0 us)
